TPU v7x, 256 devices: a whole 4x4x8 slice. The times are simulated.
256 devices in a mesh: tm: 8 (over z_lo, x), row: 4 (over z_hi), col: 8 (over y, core).
Axes of the slice: x: 4, y: 4, z: 8 (z_hi: 4, z_lo: 2; z = z_hi * 2 + z_lo), core: 2. Of those that a mesh axis runs over, the one named last changes fastest.
Arguments:
- matrix_tiles: float32 [32768, 16384], P(('tm', 'row'), 'col'), may hold values from -0.046875 to 0.046875
- block_map: int32 [128, 64], P(('tm', 'row'), 'col'), may hold values 0 or 1
- link_tiles: float32 [32768, 2048], P(('tm', 'row'), 'col'), may hold values from -0.125 to 0.125
- demand: float32 [32, 32768], P(None, ('tm', 'row')), may hold values from -6 to 6
- objective: float32 [131072], P(('tm', 'col')), may hold values from -6 to 6
- upper_bound: float32 [131072], P(('tm', 'col')), may hold values from 0.5 to 4
- restart_flag: int32 [3, 32], replicated, may hold values from 0 to 1
- step_index: int32 [3, 32], replicated, may hold values from 0 to 3
Outputs:
- primal: float32 [32, 131072], P(None, ('tm', 'col'))
- dual: float32 [32, 32768], P(None, ('tm', 'row'))
- kkt: float32 [8, 3, 32], P('tm')
Inputs may be any that keep to these rules, and one draw needn't show every extreme that they name: `restart_flag`: 1 restarts that scenario's iterates from their averages after that iteration, 0 does not.
All inputs are finite; a program needn't handle non-finite values. No bound on the sum of `block_map` on one device may be relied on, other than what follows from the above.
Results may differ from a plain program's by a relative error of at most 0.0001.
Values sent between devices are 32-bit elements; how exact they have to be, the bound alone decides.
A program may use at most 128 MiB of HBM per device.

v0:
```python
import jax
import jax.numpy as jnp
from jax import lax
from jax.sharding import PartitionSpec as P

ITERS = 3


precise = lax.Precision.HIGHEST


def from_behind(x, axis, by):
    size = lax.axis_size(axis)
    return lax.ppermute(x, axis, [(i, (i + by) % size) for i in range(size)])


def times_transpose(left, right):
    return lax.dot_general(
        left, right, (((1,), (1,)), ((), ())), precision=precise, preferred_element_type=jnp.float32
    )


def times_plain(left, right):
    return jnp.dot(left, right, precision=precise, preferred_element_type=jnp.float32)


def on_device(
    matrix_tiles, block_map, link_tiles, demand, objective, upper_bound, restart_flag, step_index
):
    rows_dev, cols_dev = matrix_tiles.shape
    stor_cols = link_tiles.shape[1]
    block_size = rows_dev // block_map.shape[0]
    scenarios = demand.shape[0]
    row_count = lax.axis_size("row")
    col_count = lax.axis_size("col")
    expanded = jnp.repeat(
        jnp.repeat(block_map.astype(jnp.float32), block_size, axis=0), block_size, axis=1
    )
    operator = matrix_tiles * expanded
    edge = cols_dev - stor_cols

    def apply_matrix(vector_in):
        previous = from_behind(vector_in[:, edge:], "tm", 1)
        partial_rows = times_transpose(vector_in, operator) + times_transpose(previous, link_tiles)
        return lax.psum(partial_rows, "col")

    def adjoint_terms(dual_in):
        main_part = times_plain(dual_in, operator)
        side_part = times_plain(dual_in, link_tiles)
        main_sum, side_sum = lax.psum((main_part, side_part), "row")
        arriving = from_behind(side_sum, "tm", -1)
        padded = jnp.concatenate([jnp.zeros((scenarios, edge), jnp.float32), arriving], axis=1)
        return main_sum + padded

    primal = jnp.zeros((scenarios, cols_dev), jnp.float32)
    dual = jnp.zeros((scenarios, rows_dev), jnp.float32)
    anchor_primal, anchor_dual = (primal, dual)
    avg_primal, avg_dual = (primal, dual)
    count = jnp.zeros((scenarios,), jnp.float32)
    weight_now = jnp.ones((scenarios,), jnp.float32)
    for iteration in range(ITERS):
        eta = 0.15 * (1.0 + step_index[iteration].astype(jnp.float32))
        tau = (eta / weight_now)[:, None]
        sigma = (eta * weight_now)[:, None]
        if iteration == 0:
            primal_next = jnp.clip(primal - tau * objective[None, :], 0.0, upper_bound[None, :])
        else:
            adjoint_now = adjoint_terms(dual)
            primal_next = jnp.clip(
                primal - tau * (objective[None, :] - adjoint_now), 0.0, upper_bound[None, :]
            )
        applied = apply_matrix(2.0 * primal_next - primal)
        dual_next = jnp.maximum(dual + sigma * (demand - applied), 0.0)
        count = count + 1.0
        avg_primal = avg_primal + (primal_next - avg_primal) / count[:, None]
        avg_dual = avg_dual + (dual_next - avg_dual) / count[:, None]
        flag = restart_flag[iteration] == 1
        if iteration < ITERS - 1:
            primal_local = jnp.sum(jnp.square(avg_primal - anchor_primal), axis=1)
            dual_local = jnp.sum(jnp.square(avg_dual - anchor_dual), axis=1)
            primal_sq = lax.psum(primal_local, ("tm", "col"))
            dual_sq = lax.psum(dual_local, ("tm", "row"))
            candidate = jnp.sqrt((dual_sq + 1e-06) / (primal_sq + 1e-06))
            weight_now = jnp.where(flag, jnp.sqrt(weight_now * candidate), weight_now)
        rows_flag = flag[:, None]
        primal = jnp.where(rows_flag, avg_primal, primal_next)
        dual = jnp.where(rows_flag, avg_dual, dual_next)
        anchor_primal = jnp.where(rows_flag, avg_primal, anchor_primal)
        anchor_dual = jnp.where(rows_flag, avg_dual, anchor_dual)
        count = jnp.where(flag, jnp.float32(0.0), count)
    applied = apply_matrix(primal)
    violation = jnp.maximum(demand - applied, 0.0)
    adjoint_last = adjoint_terms(dual)
    reduced = objective[None, :] - adjoint_last
    viol_sum = jnp.sum(jnp.square(violation), axis=1)
    dual_rows = jnp.sum(demand * dual, axis=1)
    cost_cols = jnp.sum(objective[None, :] * primal, axis=1)
    bound_cols = jnp.sum(upper_bound[None, :] * jnp.minimum(reduced, 0.0), axis=1)
    viol_sum, dual_rows = lax.psum((viol_sum, dual_rows), "row")
    cost_cols, bound_cols = lax.psum((cost_cols, bound_cols), "col")
    con_total = rows_dev * row_count
    var_total = cols_dev * col_count
    checks = jnp.stack(
        [
            jnp.sqrt(viol_sum / con_total + 1e-06),
            cost_cols / var_total,
            (dual_rows + bound_cols) / var_total,
        ],
        axis=0,
    )
    return (primal, dual, checks[None])


def solution(mesh):
    in_specs = (
        P(("tm", "row"), "col"),
        P(("tm", "row"), "col"),
        P(("tm", "row"), "col"),
        P(None, ("tm", "row")),
        P(("tm", "col")),
        P(("tm", "col")),
        P(),
        P(),
    )
    out_specs = (P(None, ("tm", "col")), P(None, ("tm", "row")), P("tm", None, None))
    return jax.shard_map(
        on_device, mesh=mesh, in_specs=in_specs, out_specs=out_specs, check_vma=False
    )
```

profile of v0, /device:TPU:1, one launch (start us, length us, event | category | flops | bytes accessed | tf_op | source)
XLA Modules:
  0.0 792.3 jit_solution(9009855571852239110)
XLA Ops:
  13.0 7.3 copy.12
  20.4 11.7 %mul.121 = f32[1024,2048]{1,0:T(8,128)} multiply(f32[1024,2048]{1,0:T(8,128)} %param.8, f32[1024,2048]{1,0:T(8,128)} %bitcast.62) | non-fusion elementwise | flops 2097152 | bytes 25165824 | tf_op jit(solution)/shard_map/mul | solution.py:39
  32.1 10.2 %fusion.1 = f32[32,1024]{1,0:T(8,128)S(1)} fusion(f32[1024,2048]{1,0:T(8,128)} %mul.121, f32[2048]{0:T(1024)S(1)} %copy-done.6, f32[32]{0:T(128)S(1)} %multiply_bitcast_fusion.2, f32[2048]{0:T(1024)S(1)} %copy-done.7), kind=kOutput, calls=%fused_computation.25 | convolution fusion | flops 805634048 | bytes 8536192 | tf_op jit(solution)/shard_map/dot_general | solution.py:18
  44.1 139.5 %psum.128 = f32[32]{0:T(128)S(1)} all-reduce(f32[32]{0:T(128)S(1)} %get-tuple-element.28), channel_id=1, replica_groups=mesh['tm'=8,'row'=4,'col'=8] {'tm','col'}, use_global_device_ids=true, to_apply=%region_4.5 | all-reduce | flops 32 | bytes 256 | tf_op jit(solution)/shard_map/psum | solution.py:81
  184.7 7.9 fusion.7
  193.2 59.4 %psum.127 = f32[32]{0:T(128)S(1)} all-reduce(f32[32]{0:T(128)S(1)} %get-tuple-element.22), channel_id=1, replica_groups=mesh['tm'=8,'row'=4,'col'=8] {'tm','row'}, use_global_device_ids=true, to_apply=%region_2.3 | all-reduce | flops 32 | bytes 256 | tf_op jit(solution)/shard_map/psum | solution.py:82
  252.7 14.2 %psum.130 = f32[32,256]{1,0:T(8,128)S(1)} all-reduce(f32[32,256]{1,0:T(8,128)S(1)} %fusion.8), channel_id=1, replica_groups=mesh['tm'=8,'row'=4,'col'=8] {'row'}, use_global_device_ids=true, to_apply=%region_6.7 | all-reduce | flops 8192 | bytes 65536 | tf_op jit(solution)/shard_map/psum | solution.py:50
  267.9 2.1 collective-permute-done.1
  271.3 5.2 collective-permute-start.2
  276.5 10.0 %fusion.9 = f32[32,1024]{1,0:T(8,128)S(1)} fusion(f32[32,2048]{1,0:T(8,128)S(1)} %get-tuple-element.27, f32[1024,2048]{1,0:T(8,128)} %mul.121), kind=kOutput, calls=%fused_computation.52 | convolution fusion | flops 805306368 | bytes 8781824 | tf_op jit(solution)/shard_map/dot_general | solution.py:18
  288.3 160.6 %psum.133 = f32[32]{0:T(128)S(1)} all-reduce(f32[32]{0:T(128)S(1)} %get-tuple-element.26), channel_id=1, replica_groups=mesh['tm'=8,'row'=4,'col'=8] {'tm','col'}, use_global_device_ids=true, to_apply=%region_11.12 | all-reduce | flops 32 | bytes 256 | tf_op jit(solution)/shard_map/psum | solution.py:81
  450.0 58.4 %psum.132 = f32[32]{0:T(128)S(1)} all-reduce(f32[32]{0:T(128)S(1)} %multiply_reduce_fusion.6), channel_id=1, replica_groups=mesh['tm'=8,'row'=4,'col'=8] {'tm','row'}, use_global_device_ids=true, to_apply=%region_9.10 | all-reduce | flops 32 | bytes 256 | tf_op jit(solution)/shard_map/psum | solution.py:82
  510.0 13.9 %psum.135 = f32[32,256]{1,0:T(8,128)S(1)} all-reduce(f32[32,256]{1,0:T(8,128)S(1)} %fusion.5), channel_id=1, replica_groups=mesh['tm'=8,'row'=4,'col'=8] {'row'}, use_global_device_ids=true, to_apply=%region_13.14 | all-reduce | flops 8192 | bytes 65536 | tf_op jit(solution)/shard_map/psum | solution.py:50
  523.9 4.5 collective-permute-start.3
  528.4 9.1 %fusion.6 = f32[32,2048]{1,0:T(8,128)} fusion(f32[1024,2048]{1,0:T(8,128)} %mul.121, pred[32]{0:T(512)(128)(4,1)S(1)} %get-tuple-element.31, f32[32,1024]{1,0:T(8,128)S(1)} %get-tuple-element.23, f32[32,1024]{1,0:T(8,128)S(1)} %copy-done.1, f32[32,1024]{1,0:T(8,128)} %all-reduce.17.cloned.1.call-done, f32[32]{0:T(128)S(1)} %get-tuple-element.20, ...), kind=kOutput, calls=%fused_computation.49 | convolution fusion | flops 805568512 | bytes 9044256 | tf_op jit(solution)/shard_map/dot_general | solution.py:24
  537.6 79.6 %all-reduce.19.cloned.1.call-done = f32[32,2048]{1,0:T(8,128)} async-done(((f32[32,2048]{1,0:T(8,128)}), f32[32,2048]{1,0:T(8,128)}) %all-reduce.19.cloned.1.call-update) | async-done | bytes 262160 | tf_op jit(solution)/shard_map/psum | solution.py:50
  618.5 10.1 %fusion.11 = f32[32,1024]{1,0:T(8,128)S(1)} fusion(f32[32,2048]{1,0:T(8,128)S(1)} %get-tuple-element.25, f32[1024,2048]{1,0:T(8,128)} %mul.121), kind=kOutput, calls=%fused_computation.54 | convolution fusion | flops 805306368 | bytes 8781824 | tf_op jit(solution)/shard_map/dot_general | solution.py:18
  630.3 10.0 %fusion.10 = f32[32,1024]{1,0:T(8,128)S(1)} fusion(f32[32,2048]{1,0:T(8,128)S(1)} %get-tuple-element.24, f32[1024,2048]{1,0:T(8,128)} %mul.121), kind=kOutput, calls=%fused_computation.53 | convolution fusion | flops 805306368 | bytes 8781824 | tf_op jit(solution)/shard_map/dot_general | solution.py:18
  647.2 62.4 %all-reduce.23.cloned.1.call-done = (f32[32,1024]{1,0:T(8,128)}, f32[32,1024]{1,0:T(8,128)}) async-done(((f32[32,1024]{1,0:T(8,128)}, f32[32,1024]{1,0:T(8,128)}), (f32[32,1024]{1,0:T(8,128)}, f32[32,1024]{1,0:T(8,128)})) %all-reduce.23.cloned.1.call-update) | async-done | bytes 262160 | tf_op jit(solution)/shard_map/psum | solution.py:45
  710.9 7.9 fusion.12
  719.5 16.8 %all-reduce.5 = (f32[32]{0:T(128)S(1)}, f32[32,256]{1,0:T(8,128)S(1)}, f32[32]{0:T(128)S(1)}) all-reduce(f32[32]{0:T(128)S(1)} %get-tuple-element.7, f32[32,256]{1,0:T(8,128)S(1)} %fusion.13, f32[32]{0:T(128)S(1)} %get-tuple-element.6), channel_id=1, replica_groups=mesh['tm'=8,'row'=4,'col'=8] {'row'}, use_global_device_ids=true, to_apply=%region_21.22 | all-reduce | flops 8256 | bytes 66048 | tf_op jit(solution)/shard_map/psum | solution.py:99
  736.2 2.6 collective-permute-start.6
  739.9 29.3 %all-reduce.21.cloned.1.call-done = f32[32,2048]{1,0:T(8,128)} async-done(((f32[32,2048]{1,0:T(8,128)}), f32[32,2048]{1,0:T(8,128)}) %all-reduce.21.cloned.1.call-update) | async-done | bytes 262160 | tf_op jit(solution)/shard_map/psum | solution.py:50
  770.3 14.3 %all-reduce.3 = (f32[32]{0:T(128)S(1)}, f32[32]{0:T(128)S(1)}) all-reduce(f32[32]{0:T(128)S(1)} %get-tuple-element.9, f32[32]{0:T(128)S(1)} %get-tuple-element.8), channel_id=1, replica_groups=mesh['tm'=8,'row'=4,'col'=8] {'col'}, use_global_device_ids=true, to_apply=%region_25.26 | all-reduce | flops 64 | bytes 512 | tf_op jit(solution)/shard_map/psum | solution.py:100
  (76 shorter events, 30.8 us)
Async XLA Ops:
  7.2 35.1 %copy-start = (f32[1024,256]{1,0:T(8,128)S(1)}, f32[1024,256]{1,0:T(8,128)}, u32[]{:S(2)}) copy-start(f32[1024,256]{1,0:T(8,128)} %param.10) | copy-start | bytes 3145732
  7.2 176.4 %all-reduce.13.cloned.1.call-start = ((), (), s32[]{:S(2)}) async-start(), calls=%async_computation | async-start | bytes 262144 | tf_op jit(solution)/shard_map/psum | solution.py:45
  9.0 33.3 %collective-permute-start = (f32[32,256]{1,0:T(8,128)S(1)}, f32[32,256]{1,0:T(8,128)S(1)}, u32[]{:S(2)}, u32[]{:S(2)}) collective-permute-start(f32[32,256]{1,0:T(8,128)S(1)} %slice.40), channel_id=1, source_target_pairs={{0,32},{32,64},{64,96},{96,128},{128,160},{160,192},{192,224},{224... | collective-permute-start | bytes 98312 | tf_op jit(solution)/shard_map/ppermute | solution.py:14
  20.4 11.7 %copy-start.6 = (f32[2048]{0:T(1024)S(1)}, f32[2048]{0:T(1024)}, u32[]{:S(2)}) copy-start(f32[2048]{0:T(1024)} %param.12) | copy-start | bytes 24580
  20.4 11.7 %copy-start.7 = (f32[2048]{0:T(1024)S(1)}, f32[2048]{0:T(1024)}, u32[]{:S(2)}) copy-start(f32[2048]{0:T(1024)} %param.13) | copy-start | bytes 24580
  32.1 12.0 %copy-start.8 = (s32[3,32]{1,0:T(4,128)S(1)}, s32[3,32]{1,0:T(4,128)}, u32[]{:S(2)}) copy-start(s32[3,32]{1,0:T(4,128)} %param.14) | copy-start | bytes 1156
  32.1 151.5 %copy-start.1 = (f32[32,1024]{1,0:T(8,128)S(1)}, f32[32,1024]{1,0:T(8,128)}, u32[]{:S(2)}) copy-start(f32[32,1024]{1,0:T(8,128)} %param.11) | copy-start | bytes 393220
  32.1 235.7 %copy-start.9 = (s32[3,32]{1,0:T(4,128)S(1)}, s32[3,32]{1,0:T(4,128)}, u32[]{:S(2)}) copy-start(s32[3,32]{1,0:T(4,128)} %param.15) | copy-start | bytes 1156
  44.1 225.9 %all-reduce.15.cloned.1.call-start = ((), (), s32[]{:S(2)}) async-start(), calls=%async_computation.1 | async-start | bytes 524288 | tf_op jit(solution)/shard_map/psum | solution.py:50
  193.2 255.7 %all-reduce.17.cloned.1.call-start = ((), (), s32[]{:S(2)}) async-start(), calls=%async_computation.2 | async-start | bytes 262144 | tf_op jit(solution)/shard_map/psum | solution.py:45
  266.9 3.1 collective-permute-start.1
  271.3 15.2 %collective-permute-start.2 = (f32[32,256]{1,0:T(8,128)S(1)}, f32[32,256]{1,0:T(8,128)S(1)}, u32[]{:S(2)}, u32[]{:S(2)}) collective-permute-start(f32[32,256]{1,0:T(8,128)S(1)} %slice.41), channel_id=1, source_target_pairs={{0,32},{32,64},{64,96},{96,128},{128,160},{160,192},{192,224},{224... | collective-permute-start | bytes 98312 | tf_op jit(solution)/shard_map/ppermute | solution.py:14
  286.5 330.7 %copy-start.5 = (f32[32,2048]{1,0:T(8,128)S(1)}, f32[32,2048]{1,0:T(8,128)}, u32[]{:S(2)}) copy-start(f32[32,2048]{1,0:T(8,128)} %all-reduce.15.cloned.1.call-done) | copy-start | bytes 786436
  288.2 329.0 %all-reduce.19.cloned.1.call-start = ((), (), s32[]{:S(2)}) async-start(), calls=%async_computation.3 | async-start | bytes 524288 | tf_op jit(solution)/shard_map/psum | solution.py:50
  523.9 13.7 %collective-permute-start.3 = (f32[32,256]{1,0:T(8,128)S(1)}, f32[32,256]{1,0:T(8,128)S(1)}, u32[]{:S(2)}, u32[]{:S(2)}) collective-permute-start(f32[32,256]{1,0:T(8,128)S(1)} %psum.135), channel_id=1, source_target_pairs={{0,224},{32,0},{64,32},{96,64},{128,96},{160,128},{192,160},{224,1... | collective-permute-start | bytes 98312 | tf_op jit(solution)/shard_map/ppermute | solution.py:14
  537.5 172.1 %all-reduce.23.cloned.1.call-start = ((), (), s32[]{:S(2)}) async-start(), calls=%async_computation.5 | async-start | bytes 524288 | tf_op jit(solution)/shard_map/psum | solution.py:45
  618.5 150.7 %copy-start.2 = (f32[32,2048]{1,0:T(8,128)}, f32[32,2048]{1,0:T(8,128)S(1)}, u32[]{:S(2)}) copy-start(f32[32,2048]{1,0:T(8,128)S(1)} %get-tuple-element.25) | copy-start | bytes 786436
  618.5 91.1 %copy-start.3 = (f32[32,1024]{1,0:T(8,128)S(1)}, f32[32,1024]{1,0:T(8,128)}, u32[]{:S(2)}) copy-start(f32[32,1024]{1,0:T(8,128)} %all-reduce.17.cloned.1.call-done) | copy-start | bytes 393220
  628.7 13.1 %collective-permute-start.5 = (f32[32,256]{1,0:T(8,128)S(1)}, f32[32,256]{1,0:T(8,128)S(1)}, u32[]{:S(2)}, u32[]{:S(2)}) collective-permute-start(f32[32,256]{1,0:T(8,128)S(1)} %slice.43), channel_id=1, source_target_pairs={{0,32},{32,64},{64,96},{96,128},{128,160},{160,192},{192,224},{224... | collective-permute-start | bytes 98312 | tf_op jit(solution)/shard_map/ppermute | solution.py:14
  640.3 5.2 collective-permute-start.4
  647.2 122.0 %all-reduce.21.cloned.1.call-start = ((), (), s32[]{:S(2)}) async-start(), calls=%async_computation.4 | async-start | bytes 524288 | tf_op jit(solution)/shard_map/psum | solution.py:50
  710.9 74.3 %copy-start.4 = (f32[32,1024]{1,0:T(8,128)}, f32[32,1024]{1,0:T(8,128)S(1)}, u32[]{:S(2)}) copy-start(f32[32,1024]{1,0:T(8,128)S(1)} %get-tuple-element.17) | copy-start | bytes 393220
  736.2 3.6 collective-permute-start.6
Sparse Core Ops, SparseCore 0:
  44.2 65.2 all-reduce.12
  193.3 50.9 all-reduce.14
  288.4 90.0 all-reduce.16
  537.7 79.5 all-reduce.18
  647.3 62.3 all-reduce.22
  719.0 50.1 all-reduce.20
where the time goes:
time: 801 us; the launch traced here: 792 us
  blocking collectives  477 us (60%)
  waiting for transfers between devices  177 us (22%)
  matrix products  74.6 us (9%)
  other arithmetic  21.4 us (3%)
  starting transfers between devices  18.7 us (2%)
  between operations  14.6 us (2%)
  local copies, waits for them, and re-layouts  9.23 us (1%)
    psum x2, blocking collectives, on_device(): primal_sq = lax.psum(primal_local, ('tm', 'col'))  300 us
    psum x2, blocking collectives, on_device(): dual_sq = lax.psum(dual_local, ('tm', 'row'))  118 us
    psum x3, waiting for transfers between devices, adjoint_terms(): main_sum, side_sum = lax.psum((main_part, side_part), 'row')  109 us
    psum x3, waiting for transfers between devices, apply_matrix(): return lax.psum(partial_rows, 'col')  62.4 us
    dot_general x8, matrix products, times_transpose(): lax.dot_general(left, right, (((1,), (1,)), ((), ())), precision=precise,...  47 us
    psum x2, blocking collectives, adjoint_terms(): main_sum, side_sum = lax.psum((main_part, side_part), 'row')  28.1 us
    dot_general x6, matrix products, times_plain(): jnp.dot(left, right, precision=precise, preferred_element_type=jnp.float32)  27.6 us
    ppermute x7, starting transfers between devices, from_behind(): return lax.ppermute(x, axis, [(i, (i + by) % size) for i in range(size)])  18.5 us
  transfers between devices with their start and end apart: 13, of which 6 were waited for; matrix products, arithmetic and copies ran while one was open for 8% of the time, Pallas kernels for 0%

commit v1 on v0

v1 whole, which is shorter than its diff:
```python
import functools

import jax
import jax.numpy as jnp
from jax import lax
from jax.experimental import pallas as pl
from jax.experimental.pallas import tpu as pltpu
from jax.sharding import PartitionSpec as P

ITERS = 3
CHUNKS = 4
LANES = 128
GROUP = 8
MESH = pl.DeviceIdType.MESH
NN = (((1,), (0,)), ((), ()))
NT = (((1,), (1,)), ((), ()))


def halves(x):
    high = x.astype(jnp.bfloat16)
    return high, (x - high.astype(jnp.float32)).astype(jnp.bfloat16)


def dot(a, b, dims):
    return lax.dot_general(a, b, dims, preferred_element_type=jnp.float32)


def product(left, high, low, dims):
    rows = left.shape[0] // 2
    both = dot(left, high, dims)
    return both[:rows] + (both[rows:] + dot(left[:rows], low, dims))


def stacked(x):
    return jnp.concatenate(halves(x), axis=0)


def column(row, start, size):
    shape = (size, row.shape[1])
    lane = lax.broadcasted_iota(jnp.int32, shape, 1)
    sub = lax.broadcasted_iota(jnp.int32, shape, 0)
    return jnp.sum(jnp.where(lane == sub + start, row, 0.0), axis=1, keepdims=True)


def spread(col, start):
    shape = (col.shape[0], LANES)
    lane = lax.broadcasted_iota(jnp.int32, shape, 1)
    sub = lax.broadcasted_iota(jnp.int32, shape, 0)
    return jnp.sum(jnp.where(lane == sub + start, col, 0.0), axis=0, keepdims=True)


def tile_of(rows):
    sub = lax.broadcasted_iota(jnp.int32, (8, LANES), 0)
    out = jnp.zeros((8, LANES), jnp.float32)
    for i, row in enumerate(rows):
        out = jnp.where(sub == i, row, out)
    return out


def kernel(
    sizes,
    mat, bmap, link, dem, obj, ub, flags, steps,
    primal_out, dual_out, kkt_out,
    kf, lf, kh, kl, lh, ll,
    ybuf, halo, pq, qb, wbuf, pa, side, ab, sb, zbuf,
    xs, xavg, xanc, ds, davg, danc, qx, qavg,
    nsend, ntm, nrow, ncol, fsend, fcol, frow,
    load_sem, out_sem,
    halo0_s, halo0_r, halo_s, halo_r, rsc_s, rsc_r, agc_s, agc_r,
    side_s, side_r, rsr_s, rsr_r, agr_s, agr_r, z_s, z_r,
    ntm_s, ntm_r, nrow_s, nrow_r, ncol_s, ncol_r, fcol_s, fcol_r, frow_s, frow_r,
):
    tms, rws, cls = sizes
    rows, cols = kf.shape
    stor = lf.shape[1]
    edge = cols - stor
    scen = dem.shape[0]
    chunk = cols // CHUNKS
    half = rows // 2
    groups = scen // GROUP
    blk = rows // bmap.shape[0]
    t, r, c = lax.axis_index("tm"), lax.axis_index("row"), lax.axis_index("col")
    g, h = lax.div(c, 2), lax.rem(c, 2)
    own_r = pl.multiple_of(r * GROUP, GROUP)
    own_g = pl.multiple_of(g * GROUP, GROUP)
    own_h = pl.multiple_of(h * half, half)
    order = [CHUNKS - 1] + list(range(CHUNKS - 1))
    pending = []

    def rem(a, n):
        return lax.rem(a, n)

    def at(tm=None, row=None, col=None):
        return {"tm": t if tm is None else tm, "row": r if row is None else row, "col": c if col is None else col}

    def send(src, dst, ssem, rsem, where):
        copy = pltpu.make_async_remote_copy(
            src_ref=src, dst_ref=dst, send_sem=ssem, recv_sem=rsem, device_id=where, device_id_type=MESH
        )
        copy.start()
        pending.append(copy)

    def arrived(dst, ssem, rsem):
        pltpu.make_async_remote_copy(
            src_ref=dst, dst_ref=dst, send_sem=ssem, recv_sem=rsem, device_id=at(), device_id_type=MESH
        ).wait_recv()

    def drain():
        for copy in pending:
            copy.wait_send()
        pending.clear()

    loads = []
    for i in range(rows // blk):
        part = pl.ds(i * blk, blk)
        loads.append(pltpu.make_async_copy(mat.at[part], kf.at[part], load_sem.at[i]))
    loads.append(pltpu.make_async_copy(link, lf, load_sem.at[rows // blk]))
    for copy in loads:
        copy.start()

    before, after = rem(t + tms - 1, tms), rem(t + 1, tms)
    barrier = pltpu.get_barrier_semaphore()
    peers = [at(tm=rem(t + d, tms)) for d in range(1, tms)]
    peers += [at(row=rem(r + d, rws)) for d in range(1, rws)]
    peers += [at(col=rem(c + d, cls)) for d in range(1, cls)]
    peers += [at(tm=x, row=rem(r + d, rws)) for x in (before, after) for d in range(1, rws)]
    for peer in peers:
        pl.semaphore_signal(barrier, inc=1, device_id=peer, device_id_type=MESH)

    weight = jnp.ones((1, scen), jnp.float32)
    count = jnp.zeros((1, scen), jnp.float32)

    def plan(k):
        eta = 0.15 * (1.0 + steps[k : k + 1, :].astype(jnp.float32))
        flag = flags[k : k + 1, :].astype(jnp.float32)
        return eta, flag

    def col_slots():
        for f in (1, 0):
            for dg in range(groups):
                if f == 0 and dg == 0:
                    continue
                hh = h if f == 0 else 1 - h
                yield dg * 2 + f, rem(g + dg, groups), hh, rem(g + groups - dg, groups)

    def send_rows_half(k, f):
        for slot, to_g, hh, _ in col_slots():
            if slot % 2 != f:
                continue
            src = pq.at[k, pl.ds(pl.multiple_of(to_g * GROUP, GROUP), GROUP), pl.ds(pl.multiple_of(hh * half, half), half)]
            send(src, qb.at[k, slot], rsc_s.at[k, slot], rsc_r.at[k, slot], at(col=to_g * 2 + hh))

    def receive_rows(k):
        total = pq[k, pl.ds(own_g, GROUP), pl.ds(own_h, half)]
        for slot, _, _, _ in col_slots():
            arrived(qb.at[k, slot], rsc_s.at[k, slot], rsc_r.at[k, slot])
            total = total + qb[k, slot]
        return total

    def dual_step(k, weight, count, eta, flag):
        sigma = column(eta * weight, own_g, GROUP)
        cnt = column(count, own_g, GROUP)
        flg = column(flag, own_g, GROUP) > 0.5
        q = receive_rows(k)
        mine = dem[pl.ds(own_g, GROUP), pl.ds(own_h, half)]
        if k == 0:
            nxt = jnp.maximum(sigma * (mine - 2.0 * q), 0.0)
            avg, qa = nxt, q
            dual = nxt
            anchor = jnp.zeros_like(nxt)
        else:
            nxt = jnp.maximum(ds[...] + sigma * (mine - (2.0 * q - qx[...])), 0.0)
            avg = davg[...] + (nxt - davg[...]) / cnt
            qa = qavg[...] + (q - qavg[...]) / cnt
            dual = jnp.where(flg, avg, nxt)
            anchor = danc[...]
        ds[...] = dual
        wbuf[k, pl.ds(own_g, GROUP), pl.ds(own_h, half)] = dual
        piece = wbuf.at[k, pl.ds(own_g, GROUP), pl.ds(own_h, half)]
        for slot, to_g, hh, _ in col_slots():
            send(piece, piece, agc_s.at[k, slot], agc_r.at[k, slot], at(col=to_g * 2 + hh))
        davg[...] = avg
        qavg[...] = qa
        q_now = jnp.where(flg, qa, q)
        qx[...] = q_now
        dist = jnp.sum(jnp.square(avg - anchor), axis=1, keepdims=True)
        danc[...] = jnp.where(flg, avg, anchor)
        if k < ITERS - 1:
            return dist
        violation = jnp.sum(jnp.square(jnp.maximum(mine - q_now, 0.0)), axis=1, keepdims=True)
        return violation, jnp.sum(mine * dual, axis=1, keepdims=True)

    def receive_dual(k):
        for slot, _, hh, from_g in col_slots():
            piece = wbuf.at[
                k, pl.ds(pl.multiple_of(from_g * GROUP, GROUP), GROUP), pl.ds(pl.multiple_of(hh * half, half), half)
            ]
            arrived(piece, agc_s.at[k, slot], agc_r.at[k, slot])

    def adjoint_side(k, left):
        side[k] = product(left, lh[...], ll[...], NN)
        for d in range(rws):
            to_r = rem(r + d, rws)
            src = side.at[k, pl.ds(pl.multiple_of(to_r * GROUP, GROUP), GROUP)]
            send(src, sb.at[k, d], side_s.at[k, d], side_r.at[k, d], at(tm=before, row=to_r))

    def adjoint_chunk(k, j, left):
        part = pl.ds(j * chunk, chunk)
        pa[k, :, part] = product(left, kh[:, part], kl[:, part], NN)
        for d in (2, 1, 3):
            to_r = rem(r + d, rws)
            src = pa.at[k, pl.ds(pl.multiple_of(to_r * GROUP, GROUP), GROUP), part]
            send(src, ab.at[k, d, :, part], rsr_s.at[k, j, d], rsr_r.at[k, j, d], at(row=to_r))

    def receive_adjoint(k, j):
        part = pl.ds(j * chunk, chunk)
        total = pa[k, pl.ds(own_r, GROUP), part]
        for d in (1, 3, 2):
            arrived(ab.at[k, d, :, part], rsr_s.at[k, j, d], rsr_r.at[k, j, d])
            total = total + ab[k, d, :, part]
        if j == CHUNKS - 1:
            extra = None
            for d in range(rws):
                arrived(sb.at[k, d], side_s.at[k, d], side_r.at[k, d])
                extra = sb[k, d] if extra is None else extra + sb[k, d]
            total = jnp.concatenate([total[:, : chunk - stor], total[:, chunk - stor :] + extra], axis=1)
        return total

    def primal_steps(k, weight, eta):
        tau = column(eta / weight, own_r, GROUP)
        for j in order:
            part = pl.ds(j * chunk, chunk)
            reduced = obj[:, part] - receive_adjoint(k - 1, j)
            ybuf[k, pl.ds(own_r, GROUP), part] = jnp.clip(xs[:, part] - tau * reduced, 0.0, ub[:, part])
            piece = ybuf.at[k, pl.ds(own_r, GROUP), part]
            for d in (2, 1, 3):
                send(piece, piece, agr_s.at[k, j, d], agr_r.at[k, j, d], at(row=rem(r + d, rws)))
            if j == CHUNKS - 1:
                for d in range(rws):
                    send(
                        ybuf.at[k, pl.ds(own_r, GROUP), pl.ds(edge, stor)],
                        halo.at[k, pl.ds(own_r, GROUP)],
                        halo_s.at[k, d], halo_r.at[k, d], at(tm=after, row=rem(r + d, rws)),
                    )

    def primal_rest(k, count, flag):
        cnt = column(count, own_r, GROUP)
        flg = column(flag, own_r, GROUP) > 0.5
        nxt = ybuf[k, pl.ds(own_r, GROUP), :]
        if k == 0:
            avg = nxt
            anchor = jnp.zeros_like(nxt)
        else:
            avg = xavg[...] + (nxt - xavg[...]) / cnt
            anchor = xanc[...]
        now = jnp.where(flg, avg, nxt)
        xs[...] = now
        xavg[...] = avg
        dist = jnp.sum(jnp.square(avg - anchor), axis=1, keepdims=True)
        xanc[...] = jnp.where(flg, avg, anchor)
        if k < ITERS - 1:
            return dist
        zbuf[pl.ds(own_r, GROUP), :] = now
        piece = zbuf.at[pl.ds(own_r, GROUP)]
        for d in (2, 1, 3):
            send(piece, piece, z_s.at[d], z_r.at[d], at(row=rem(r + d, rws)))
        return jnp.sum(obj[...] * now, axis=1, keepdims=True)

    def receive_primal(k, j):
        part = pl.ds(j * chunk, chunk)
        for d in (1, 3, 2):
            piece = ybuf.at[k, pl.ds(pl.multiple_of(rem(r + rws - d, rws) * GROUP, GROUP), GROUP), part]
            arrived(piece, agr_s.at[k, j, d], agr_r.at[k, j, d])

    def apply_chunks(k):
        acc = None
        for j in order:
            receive_primal(k, j)
            part = pl.ds(j * chunk, chunk)
            left = stacked(ybuf[k, :, part])
            if j != order[-1]:
                term = product(left, kh[:, part], kl[:, part], NT)
                if j == CHUNKS - 1:
                    for d in range(rws):
                        from_r = pl.multiple_of(rem(r + rws - d, rws) * GROUP, GROUP)
                        arrived(halo.at[k, pl.ds(from_r, GROUP)], halo_s.at[k, d], halo_r.at[k, d])
                    pq[k] = term + product(stacked(halo[k]), lh[...], ll[...], NT)
                else:
                    pq[k] = pq[k] + term
            else:
                for f in (1, 0):
                    hh = pl.multiple_of((h if f == 0 else 1 - h) * half, half)
                    some = pl.ds(hh, half)
                    pq[k, :, some] = pq[k, :, some] + product(left, kh[some, part], kl[some, part], NT)
                    send_rows_half(k, f)

    def norm_tm(k, dx, dy):
        nsend[k, 0] = tile_of([spread(dx, own_r), spread(dy, own_g)])
        for d in range(1, tms):
            send(nsend.at[k, 0], ntm.at[k, d], ntm_s.at[k, d], ntm_r.at[k, d], at(tm=rem(t + d, tms)))

    def norm_row(k):
        total = nsend[k, 0]
        for d in range(1, tms):
            arrived(ntm.at[k, d], ntm_s.at[k, d], ntm_r.at[k, d])
            total = total + ntm[k, d]
        nsend[k, 1] = total
        for d in range(1, rws):
            send(nsend.at[k, 1], nrow.at[k, d], nrow_s.at[k, d], nrow_r.at[k, d], at(row=rem(r + d, rws)))

    def norm_col(k):
        total = nsend[k, 1]
        for d in range(1, rws):
            arrived(nrow.at[k, d], nrow_s.at[k, d], nrow_r.at[k, d])
            total = total + nrow[k, d]
        nsend[k, 2] = total
        for d in range(1, cls):
            send(nsend.at[k, 2], ncol.at[k, d], ncol_s.at[k, d], ncol_r.at[k, d], at(col=rem(c + d, cls)))

    def norm_weight(k, weight, flag):
        total = nsend[k, 2]
        for d in range(1, cls):
            arrived(ncol.at[k, d], ncol_s.at[k, d], ncol_r.at[k, d])
            total = total + ncol[k, d]
        dx, dy = total[0:1, 0:scen], total[1:2, 0:scen]
        candidate = jnp.sqrt((dy + 1e-06) / (dx + 1e-06))
        return jnp.where(flag > 0.5, jnp.sqrt(weight * candidate), weight)

    eta, flag = plan(0)
    count = count + 1.0
    tau_all = column(eta, 0, scen)
    ybuf[0] = jnp.clip(-tau_all * obj[...], 0.0, ub[...])
    left0 = stacked(ybuf[0])
    for i in range(rows // blk):
        loads[i].wait()
        part = pl.ds(i * blk, blk)
        for j in range(cols // blk):
            across = pl.ds(j * blk, blk)
            high, low = halves(kf[part, across] * bmap[i, j].astype(jnp.float32))
            kh[part, across] = high
            kl[part, across] = low
        if i == 0:
            pl.semaphore_wait(barrier, len(peers))
            send(ybuf.at[0, :, pl.ds(edge, stor)], halo.at[0], halo0_s, halo0_r, at(tm=after))
        pq[0, :, part] = product(left0, kh[part, :], kl[part, :], NT)
    loads[-1].wait()
    high, low = halves(lf[...])
    lh[...] = high
    ll[...] = low
    arrived(halo.at[0], halo0_s, halo0_r)
    left0 = stacked(halo[0])
    for f in (1, 0):
        some = pl.ds(pl.multiple_of((h if f == 0 else 1 - h) * half, half), half)
        pq[0, :, some] = pq[0, :, some] + product(left0, lh[some, :], ll[some, :], NT)
        send_rows_half(0, f)
    dx = primal_rest(0, count, flag)

    for k in range(ITERS):
        if k > 0:
            eta, flag = plan(k)
            count = count + 1.0
            primal_steps(k, weight, eta)
            dx = primal_rest(k, count, flag)
            apply_chunks(k)
        if k < ITERS - 1:
            dy = dual_step(k, weight, count, eta, flag)
            norm_tm(k, dx, dy)
        else:
            viol, dual_part = dual_step(k, weight, count, eta, flag)
        drain_now, pending[:] = pending[:], []
        receive_dual(k)
        left = stacked(wbuf[k])
        adjoint_side(k, left)
        for n, j in enumerate(order):
            adjoint_chunk(k, j, left)
            if k < ITERS - 1 and n == 1:
                norm_row(k)
        for copy in drain_now:
            copy.wait_send()
        if k < ITERS - 1:
            norm_col(k)
            weight = norm_weight(k, weight, flag)
            count = jnp.where(flag > 0.5, 0.0, count)

    k = ITERS - 1
    dual_copy = pltpu.make_async_copy(wbuf.at[k], dual_out, out_sem.at[0])
    dual_copy.start()
    for d in (1, 3, 2):
        from_r = pl.multiple_of(rem(r + rws - d, rws) * GROUP, GROUP)
        arrived(zbuf.at[pl.ds(from_r, GROUP)], z_s.at[d], z_r.at[d])
    primal_copy = pltpu.make_async_copy(zbuf, primal_out, out_sem.at[1])
    primal_copy.start()
    bound = jnp.zeros((GROUP, 1), jnp.float32)
    for j in order:
        part = pl.ds(j * chunk, chunk)
        reduced = obj[:, part] - receive_adjoint(k, j)
        bound = bound + jnp.sum(ub[:, part] * jnp.minimum(reduced, 0.0), axis=1, keepdims=True)
    cost = dx
    fcol[c] = tile_of([spread(viol, own_g), spread(dual_part, own_g), spread(cost, own_r), spread(bound, own_r)])
    for d in range(1, cls):
        send(fcol.at[c], fcol.at[c], fcol_s.at[d], fcol_r.at[d], at(col=rem(c + d, cls)))
    drain_now, pending[:] = pending[:], []
    for d in range(1, cls):
        arrived(fcol.at[rem(c + cls - d, cls)], fcol_s.at[d], fcol_r.at[d])
    total = fcol[0]
    for i in range(1, cls):
        total = total + fcol[i]
    frow[r] = total
    for d in range(1, rws):
        send(frow.at[r], frow.at[r], frow_s.at[d], frow_r.at[d], at(row=rem(r + d, rws)))
    for copy in drain_now:
        copy.wait_send()
    for d in range(1, rws):
        arrived(frow.at[rem(r + rws - d, rws)], frow_s.at[d], frow_r.at[d])
    total = frow[0]
    for i in range(1, rws):
        total = total + frow[i]
    con_total, var_total = float(rows * rws), float(cols * cls)
    kkt_out[0, 0:1, :] = jnp.sqrt(total[0:1, 0:scen] / con_total + 1e-06)
    kkt_out[0, 1:2, :] = total[2:3, 0:scen] / var_total
    kkt_out[0, 2:3, :] = (total[1:2, 0:scen] + total[3:4, 0:scen]) / var_total
    drain()
    dual_copy.wait()
    primal_copy.wait()


def on_device(matrix_tiles, block_map, link_tiles, demand, objective, upper_bound, restart_flag, step_index):
    rows, cols = matrix_tiles.shape
    stor = link_tiles.shape[1]
    scen = demand.shape[0]
    tms, rws, cls = lax.axis_size("tm"), lax.axis_size("row"), lax.axis_size("col")
    half = rows // 2
    f32, bf16 = jnp.float32, jnp.bfloat16
    vmem = pl.BlockSpec(memory_space=pltpu.VMEM)
    smem = pl.BlockSpec(memory_space=pltpu.SMEM)
    anywhere = pl.BlockSpec(memory_space=pl.ANY)
    V = pltpu.VMEM
    D = pltpu.SemaphoreType.DMA
    n = ITERS
    scratch = [
        V((rows, cols), f32), V((rows, stor), f32),
        V((rows, cols), bf16), V((rows, cols), bf16), V((rows, stor), bf16), V((rows, stor), bf16),
        V((n, scen, cols), f32), V((n, scen, stor), f32), V((n, scen, rows), f32), V((n, cls, GROUP, half), f32),
        V((n, scen, rows), f32), V((n, scen, cols), f32), V((n, scen, stor), f32),
        V((n, rws, GROUP, cols), f32), V((n, rws, GROUP, stor), f32), V((scen, cols), f32),
        V((GROUP, cols), f32), V((GROUP, cols), f32), V((GROUP, cols), f32),
        V((GROUP, half), f32), V((GROUP, half), f32), V((GROUP, half), f32), V((GROUP, half), f32), V((GROUP, half), f32),
        V((n - 1, 3, 8, LANES), f32), V((n - 1, tms, 8, LANES), f32), V((n - 1, rws, 8, LANES), f32),
        V((n - 1, cls, 8, LANES), f32), V((8, LANES), f32), V((cls, 8, LANES), f32), V((rws, 8, LANES), f32),
        D((rows // (rows // block_map.shape[0]) + 1,)), D((2,)),
        D(()), D(()), D((n, rws)), D((n, rws)), D((n, cls)), D((n, cls)), D((n, cls)), D((n, cls)),
        D((n, rws)), D((n, rws)), D((n, CHUNKS, rws)), D((n, CHUNKS, rws)),
        D((n, CHUNKS, rws)), D((n, CHUNKS, rws)), D((rws,)), D((rws,)),
        D((n - 1, tms)), D((n - 1, tms)), D((n - 1, rws)), D((n - 1, rws)), D((n - 1, cls)), D((n - 1, cls)),
        D((cls,)), D((cls,)), D((rws,)), D((rws,)),
    ]
    return pl.pallas_call(
        functools.partial(kernel, (tms, rws, cls)),
        out_shape=(
            jax.ShapeDtypeStruct((scen, cols), f32),
            jax.ShapeDtypeStruct((scen, rows), f32),
            jax.ShapeDtypeStruct((1, 3, scen), f32),
        ),
        in_specs=[anywhere, smem, anywhere, vmem, vmem, vmem, vmem, vmem],
        out_specs=(anywhere, anywhere, vmem),
        scratch_shapes=scratch,
        compiler_params=pltpu.CompilerParams(
            collective_id=0, has_side_effects=True, vmem_limit_bytes=48 << 20
        ),
        name="pdhg",
    )(
        matrix_tiles, block_map, link_tiles, demand, objective.reshape(1, cols), upper_bound.reshape(1, cols),
        restart_flag, step_index,
    )


def solution(mesh):
    in_specs = (
        P(("tm", "row"), "col"),
        P(("tm", "row"), "col"),
        P(("tm", "row"), "col"),
        P(None, ("tm", "row")),
        P(("tm", "col")),
        P(("tm", "col")),
        P(),
        P(),
    )
    out_specs = (P(None, ("tm", "col")), P(None, ("tm", "row")), P("tm", None, None))
    return jax.shard_map(
        on_device, mesh=mesh, in_specs=in_specs, out_specs=out_specs, check_vma=False
    )
```

time: 801 us -> 121 us (0.15); the launches traced: 792 us -> 121 us
  blocking collectives: 477 us -> 0 us
  waiting for transfers between devices: 177 us -> 0 us
  Pallas kernels: 0 us -> 112 us
  matrix products: 74.6 us -> 0 us
  other arithmetic: 21.4 us -> 0 us
  starting transfers between devices: 18.7 us -> 0 us
  between operations: 14.6 us -> 0.66 us
    psum x8 -> x0, blocking collectives: 477 us -> none  [the longest x2 300 us: on_device(): primal_sq = lax.psum(primal_local, ('tm', 'col'))]
    psum x6 -> x0, waiting for transfers between devices: 171 us -> none  [the longest x3 109 us: adjoint_terms(): main_sum, side_sum = lax.psum((main_part, side_part), 'row')]
    pallas_call x0 -> x1, Pallas kernels: none -> 112 us  [on_device(): pl.pallas_call(functools.partial(kernel, (tms, rws, cls)), out_shape=(jax...]
    dot_general x14 -> x0, matrix products: 74.6 us -> none  [the longest x8 47 us: times_transpose(): lax.dot_general(left, right, (((1,), (1,)), ((), ())), precision=precise,...]
    ppermute x7 -> x0, starting transfers between devices: 18.5 us -> none  [from_behind(): return lax.ppermute(x, axis, [(i, (i + by) % size) for i in range(size)])]
    mul x4 -> x0, other arithmetic: 12.5 us -> none  [the longest x1 11.7 us: on_device(): operator = matrix_tiles * expanded]
  transfers between devices with their start and end apart: 13 -> 0, of which waited for: 6 -> 0; matrix products, arithmetic and copies ran while one was open for 8% -> 0% of each run, Pallas kernels for 0% -> 0%
where the time goes in v1:
time: 121 us
  Pallas kernels  112 us (93%)
  local copies, waits for them, and re-layouts  7.48 us (6%)
    pallas_call x1, Pallas kernels, on_device(): pl.pallas_call(functools.partial(kernel, (tms, rws, cls)), out_shape=(jax...  112 us
    unnamed x16, local copies, waits for them, and re-layouts  6.91 us

profile of v1, /device:TPU:1, one launch (start us, length us, event | category | flops | bytes accessed | tf_op | source)
XLA Modules:
  0.0 120.5 jit_solution(14632491230393803668)
XLA Ops:
  0.6 0.0 copy-start
  0.6 1.2 %copy-done = f32[1024,256]{1,0:T(8,128)S(1)} copy-done((f32[1024,256]{1,0:T(8,128)S(1)}, f32[1024,256]{1,0:T(8,128)}, u32[]{:S(2)}) %copy-start) | copy-done | bytes 1048600
  1.9 0.0 copy-start.1
  1.9 0.9 copy-done.1
  2.8 0.0 copy-start.2
  2.8 0.7 copy-done.2
  3.5 0.0 copy-start.3
  3.5 0.7 copy-done.3
  4.2 0.0 copy-start.4
  4.2 0.7 copy-done.4
  4.8 0.0 copy-start.5
  4.8 0.7 copy-done.5
  5.5 0.0 copy-start.6
  5.5 0.7 copy-done.6
  6.2 112.4 %pdhg.1 = (f32[32,2048]{1,0:T(8,128)S(1)}, f32[32,1024]{1,0:T(8,128)S(1)}, f32[1,3,32]{2,1,0:T(4,128)S(1)}) custom-call(f32[1024,2048]{1,0:T(8,128)} %mat.1, s32[4,8]{1,0:T(4,128)S(1)} %copy-done.4, f32[1024,256]{1,0:T(8,128)S(1)} %copy-done, f32[32,1024]{1,0:T(8,128)S(1)} %copy-done.1, f32[1,2048]{1,0:T(1,128)S(1)} %bitcast.2, f32[1,2048]{1,0:T(1,128)S(1)} %bitcast.3, ...), custom_call_target="tpu_custom_call" | custom-call | tf_op jit(solution)/shard_map/pdhg/pallas_call | solution.py:457
  118.6 0.6 copy.11
  119.2 0.7 copy.14
  119.9 0.7 copy.15
Async XLA Ops:
  0.6 1.2 %copy-start = (f32[1024,256]{1,0:T(8,128)S(1)}, f32[1024,256]{1,0:T(8,128)}, u32[]{:S(2)}) copy-start(f32[1024,256]{1,0:T(8,128)} %link.1) | copy-start | bytes 3145732
  1.9 0.9 copy-start.1
  2.8 0.7 copy-start.2
  3.5 0.7 copy-start.3
  4.2 0.7 copy-start.4
  4.8 0.7 copy-start.5
  5.5 0.7 copy-start.6

commit v2 on v1

--- a/solution.py
+++ b/solution.py
@@ -49,41 +49,37 @@
     return jnp.sum(jnp.where(lane == sub + start, col, 0.0), axis=0, keepdims=True)
 
 
-def tile_of(rows):
-    sub = lax.broadcasted_iota(jnp.int32, (8, LANES), 0)
-    out = jnp.zeros((8, LANES), jnp.float32)
-    for i, row in enumerate(rows):
-        out = jnp.where(sub == i, row, out)
-    return out
-
-
 def kernel(
     sizes,
-    mat, bmap, link, dem, obj, ub, flags, steps,
+    mat, bmap_in, link, dem_in, obj_in, ub_in, flags_in, steps_in,
     primal_out, dual_out, kkt_out,
+    bmap, flags, steps, dem, costs, far,
     kf, lf, kh, kl, lh, ll,
-    ybuf, halo, pq, qb, wbuf, pa, side, ab, sb, zbuf,
+    ybuf, ypiece, halo, pq, qb, wbuf, pa, side, ab, sb, zbuf, zpiece,
     xs, xavg, xanc, ds, davg, danc, qx, qavg,
-    nsend, ntm, nrow, ncol, fsend, fcol, frow,
-    load_sem, out_sem,
-    halo0_s, halo0_r, halo_s, halo_r, rsc_s, rsc_r, agc_s, agc_r,
+    nsend, near_buf, wide_buf, fpart, fcol, fsum, frow,
+    load_sem, small_sem, out_sem, pair_sem,
+    halo_s, halo_r, rsc_s, rsc_r, agc_s, agc_r,
     side_s, side_r, rsr_s, rsr_r, agr_s, agr_r, z_s, z_r,
-    ntm_s, ntm_r, nrow_s, nrow_r, ncol_s, ncol_r, fcol_s, fcol_r, frow_s, frow_r,
+    near_s, near_r, wide_s, wide_r, fcol_s, fcol_r, frow_s, frow_r,
 ):
     tms, rws, cls = sizes
     rows, cols = kf.shape
     stor = lf.shape[1]
     edge = cols - stor
-    scen = dem.shape[0]
+    scen = ybuf.shape[1]
     chunk = cols // CHUNKS
     half = rows // 2
     groups = scen // GROUP
     blk = rows // bmap.shape[0]
     t, r, c = lax.axis_index("tm"), lax.axis_index("row"), lax.axis_index("col")
     g, h = lax.div(c, 2), lax.rem(c, 2)
+    o = lax.rem(t + tms // 2, tms)
     own_r = pl.multiple_of(r * GROUP, GROUP)
     own_g = pl.multiple_of(g * GROUP, GROUP)
     own_h = pl.multiple_of(h * half, half)
+    near_first = (0, 1, 3, 2)
+    far_first = near_first[::-1]
     order = [CHUNKS - 1] + list(range(CHUNKS - 1))
     pending = []
 
@@ -110,20 +106,41 @@
             copy.wait_send()
         pending.clear()
 
+    small = [
+        pltpu.make_async_copy(src, dst, small_sem.at[i])
+        for i, (src, dst) in enumerate(
+            (
+                (steps_in, steps), (obj_in, costs.at[0]), (ub_in, costs.at[1]), (bmap_in, bmap), (flags_in, flags),
+                (dem_in.at[pl.ds(own_g, GROUP), pl.ds(own_h, half)], dem),
+            )
+        )
+    ]
     loads = []
     for i in range(rows // blk):
         part = pl.ds(i * blk, blk)
         loads.append(pltpu.make_async_copy(mat.at[part], kf.at[part], load_sem.at[i]))
     loads.append(pltpu.make_async_copy(link, lf, load_sem.at[rows // blk]))
-    for copy in loads:
+    for copy in small + loads:
         copy.start()
 
-    before, after = rem(t + tms - 1, tms), rem(t + 1, tms)
+    def near_peers():
+        for dt in range(tms):
+            for f in range(2):
+                if dt or f:
+                    yield dt * 2 + f, at(tm=rem(t + dt, tms), col=g * 2 + (1 - h if f else h))
+
+    def wide_peers():
+        for dr in (2, 1, 3, 0):
+            for dg in range(groups):
+                if dr or dg:
+                    yield dr * groups + dg, at(row=rem(r + dr, rws), col=rem(g + dg, groups) * 2 + h)
+
+    behind, ahead = rem(o + tms - 1, tms), rem(o + 1, tms)
     barrier = pltpu.get_barrier_semaphore()
-    peers = [at(tm=rem(t + d, tms)) for d in range(1, tms)]
-    peers += [at(row=rem(r + d, rws)) for d in range(1, rws)]
-    peers += [at(col=rem(c + d, cls)) for d in range(1, cls)]
-    peers += [at(tm=x, row=rem(r + d, rws)) for x in (before, after) for d in range(1, rws)]
+    peers = [at(tm=x, row=rem(r + d, rws)) for d in (2, 1, 3) for x in (o, behind, ahead)]
+    peers += [place for _, place in wide_peers()]
+    peers += [place for _, place in near_peers()]
+    peers += [at(col=rem(g + dg, groups) * 2 + 1 - h) for dg in range(1, groups)]
     for peer in peers:
         pl.semaphore_signal(barrier, inc=1, device_id=peer, device_id_type=MESH)
 
@@ -162,7 +179,7 @@
         cnt = column(count, own_g, GROUP)
         flg = column(flag, own_g, GROUP) > 0.5
         q = receive_rows(k)
-        mine = dem[pl.ds(own_g, GROUP), pl.ds(own_h, half)]
+        mine = dem[...]
         if k == 0:
             nxt = jnp.maximum(sigma * (mine - 2.0 * q), 0.0)
             avg, qa = nxt, q
@@ -202,22 +219,22 @@
         for d in range(rws):
             to_r = rem(r + d, rws)
             src = side.at[k, pl.ds(pl.multiple_of(to_r * GROUP, GROUP), GROUP)]
-            send(src, sb.at[k, d], side_s.at[k, d], side_r.at[k, d], at(tm=before, row=to_r))
+            send(src, sb.at[k, d], side_s.at[k, d], side_r.at[k, d], at(tm=behind, row=to_r))
 
     def adjoint_chunk(k, j, left):
         part = pl.ds(j * chunk, chunk)
         pa[k, :, part] = product(left, kh[:, part], kl[:, part], NN)
-        for d in (2, 1, 3):
+        for d in far_first:
             to_r = rem(r + d, rws)
             src = pa.at[k, pl.ds(pl.multiple_of(to_r * GROUP, GROUP), GROUP), part]
-            send(src, ab.at[k, d, :, part], rsr_s.at[k, j, d], rsr_r.at[k, j, d], at(row=to_r))
+            send(src, ab.at[k, d, :, part], rsr_s.at[k, j, d], rsr_r.at[k, j, d], at(tm=o, row=to_r))
 
     def receive_adjoint(k, j):
         part = pl.ds(j * chunk, chunk)
-        total = pa[k, pl.ds(own_r, GROUP), part]
-        for d in (1, 3, 2):
+        total = None
+        for d in near_first:
             arrived(ab.at[k, d, :, part], rsr_s.at[k, j, d], rsr_r.at[k, j, d])
-            total = total + ab[k, d, :, part]
+            total = ab[k, d, :, part] if total is None else total + ab[k, d, :, part]
         if j == CHUNKS - 1:
             extra = None
             for d in range(rws):
@@ -230,23 +247,24 @@
         tau = column(eta / weight, own_r, GROUP)
         for j in order:
             part = pl.ds(j * chunk, chunk)
-            reduced = obj[:, part] - receive_adjoint(k - 1, j)
-            ybuf[k, pl.ds(own_r, GROUP), part] = jnp.clip(xs[:, part] - tau * reduced, 0.0, ub[:, part])
-            piece = ybuf.at[k, pl.ds(own_r, GROUP), part]
-            for d in (2, 1, 3):
-                send(piece, piece, agr_s.at[k, j, d], agr_r.at[k, j, d], at(row=rem(r + d, rws)))
+            reduced = far[0, :, part] - receive_adjoint(k - 1, j)
+            ypiece[k, :, part] = jnp.clip(xs[:, part] - tau * reduced, 0.0, far[1, :, part])
+            for d in far_first:
+                send(
+                    ypiece.at[k, :, part], ybuf.at[k, pl.ds(own_r, GROUP), part],
+                    agr_s.at[k, j, d], agr_r.at[k, j, d], at(tm=o, row=rem(r + d, rws)),
+                )
             if j == CHUNKS - 1:
-                for d in range(rws):
+                for d in far_first:
                     send(
-                        ybuf.at[k, pl.ds(own_r, GROUP), pl.ds(edge, stor)],
-                        halo.at[k, pl.ds(own_r, GROUP)],
-                        halo_s.at[k, d], halo_r.at[k, d], at(tm=after, row=rem(r + d, rws)),
+                        ypiece.at[k, :, pl.ds(edge, stor)], halo.at[k, pl.ds(own_r, GROUP)],
+                        halo_s.at[k, d], halo_r.at[k, d], at(tm=ahead, row=rem(r + d, rws)),
                     )
 
     def primal_rest(k, count, flag):
         cnt = column(count, own_r, GROUP)
         flg = column(flag, own_r, GROUP) > 0.5
-        nxt = ybuf[k, pl.ds(own_r, GROUP), :]
+        nxt = ypiece[k]
         if k == 0:
             avg = nxt
             anchor = jnp.zeros_like(nxt)
@@ -260,15 +278,14 @@
         xanc[...] = jnp.where(flg, avg, anchor)
         if k < ITERS - 1:
             return dist
-        zbuf[pl.ds(own_r, GROUP), :] = now
-        piece = zbuf.at[pl.ds(own_r, GROUP)]
-        for d in (2, 1, 3):
-            send(piece, piece, z_s.at[d], z_r.at[d], at(row=rem(r + d, rws)))
-        return jnp.sum(obj[...] * now, axis=1, keepdims=True)
+        zpiece[...] = now
+        for d in far_first:
+            send(zpiece, zbuf.at[pl.ds(own_r, GROUP)], z_s.at[d], z_r.at[d], at(tm=o, row=rem(r + d, rws)))
+        return jnp.sum(far[0] * now, axis=1, keepdims=True)
 
     def receive_primal(k, j):
         part = pl.ds(j * chunk, chunk)
-        for d in (1, 3, 2):
+        for d in near_first:
             piece = ybuf.at[k, pl.ds(pl.multiple_of(rem(r + rws - d, rws) * GROUP, GROUP), GROUP), part]
             arrived(piece, agr_s.at[k, j, d], agr_r.at[k, j, d])
 
@@ -294,42 +311,34 @@
                     pq[k, :, some] = pq[k, :, some] + product(left, kh[some, part], kl[some, part], NT)
                     send_rows_half(k, f)
 
-    def norm_tm(k, dx, dy):
-        nsend[k, 0] = tile_of([spread(dx, own_r), spread(dy, own_g)])
-        for d in range(1, tms):
-            send(nsend.at[k, 0], ntm.at[k, d], ntm_s.at[k, d], ntm_r.at[k, d], at(tm=rem(t + d, tms)))
-
-    def norm_row(k):
+    def norm_start(k, dx, dy):
+        nsend[k, 0] = spread(dx, own_r) + spread(dy, scen + own_g)
+        for slot, place in near_peers():
+            send(nsend.at[k, 0], near_buf.at[k, slot], near_s.at[k, slot], near_r.at[k, slot], place)
+
+    def norm_middle(k):
         total = nsend[k, 0]
-        for d in range(1, tms):
-            arrived(ntm.at[k, d], ntm_s.at[k, d], ntm_r.at[k, d])
-            total = total + ntm[k, d]
+        for slot, _ in near_peers():
+            arrived(near_buf.at[k, slot], near_s.at[k, slot], near_r.at[k, slot])
+            total = total + near_buf[k, slot]
         nsend[k, 1] = total
-        for d in range(1, rws):
-            send(nsend.at[k, 1], nrow.at[k, d], nrow_s.at[k, d], nrow_r.at[k, d], at(row=rem(r + d, rws)))
-
-    def norm_col(k):
+        for slot, place in wide_peers():
+            send(nsend.at[k, 1], wide_buf.at[k, slot], wide_s.at[k, slot], wide_r.at[k, slot], place)
+
+    def norm_weight(k, weight, flag):
         total = nsend[k, 1]
-        for d in range(1, rws):
-            arrived(nrow.at[k, d], nrow_s.at[k, d], nrow_r.at[k, d])
-            total = total + nrow[k, d]
-        nsend[k, 2] = total
-        for d in range(1, cls):
-            send(nsend.at[k, 2], ncol.at[k, d], ncol_s.at[k, d], ncol_r.at[k, d], at(col=rem(c + d, cls)))
-
-    def norm_weight(k, weight, flag):
-        total = nsend[k, 2]
-        for d in range(1, cls):
-            arrived(ncol.at[k, d], ncol_s.at[k, d], ncol_r.at[k, d])
-            total = total + ncol[k, d]
-        dx, dy = total[0:1, 0:scen], total[1:2, 0:scen]
+        for slot, _ in wide_peers():
+            arrived(wide_buf.at[k, slot], wide_s.at[k, slot], wide_r.at[k, slot])
+            total = total + wide_buf[k, slot]
+        dx, dy = total[:, 0:scen], total[:, scen : 2 * scen]
         candidate = jnp.sqrt((dy + 1e-06) / (dx + 1e-06))
         return jnp.where(flag > 0.5, jnp.sqrt(weight * candidate), weight)
 
+    for copy in small:
+        copy.wait()
     eta, flag = plan(0)
     count = count + 1.0
-    tau_all = column(eta, 0, scen)
-    ybuf[0] = jnp.clip(-tau_all * obj[...], 0.0, ub[...])
+    ybuf[0] = jnp.clip(-column(eta, 0, scen) * costs[0], 0.0, costs[1])
     left0 = stacked(ybuf[0])
     for i in range(rows // blk):
         loads[i].wait()
@@ -339,20 +348,23 @@
             high, low = halves(kf[part, across] * bmap[i, j].astype(jnp.float32))
             kh[part, across] = high
             kl[part, across] = low
-        if i == 0:
+        pq[0, :, part] = product(left0, kh[part, :], kl[part, :], NT)
+        if i == 1:
             pl.semaphore_wait(barrier, len(peers))
-            send(ybuf.at[0, :, pl.ds(edge, stor)], halo.at[0], halo0_s, halo0_r, at(tm=after))
-        pq[0, :, part] = product(left0, kh[part, :], kl[part, :], NT)
+            send(ybuf.at[0, :, pl.ds(edge, stor)], halo.at[0], pair_sem.at[0], pair_sem.at[1], at(tm=rem(t + 1, tms)))
+            send(costs, far, pair_sem.at[2], pair_sem.at[3], at(tm=o))
     loads[-1].wait()
     high, low = halves(lf[...])
     lh[...] = high
     ll[...] = low
-    arrived(halo.at[0], halo0_s, halo0_r)
+    arrived(halo.at[0], pair_sem.at[0], pair_sem.at[1])
     left0 = stacked(halo[0])
     for f in (1, 0):
         some = pl.ds(pl.multiple_of((h if f == 0 else 1 - h) * half, half), half)
         pq[0, :, some] = pq[0, :, some] + product(left0, lh[some, :], ll[some, :], NT)
         send_rows_half(0, f)
+    arrived(far, pair_sem.at[2], pair_sem.at[3])
+    ypiece[0] = jnp.clip(-column(eta, own_r, GROUP) * far[0], 0.0, far[1])
     dx = primal_rest(0, count, flag)
 
     for k in range(ITERS):
@@ -364,64 +376,69 @@
             apply_chunks(k)
         if k < ITERS - 1:
             dy = dual_step(k, weight, count, eta, flag)
-            norm_tm(k, dx, dy)
+            norm_start(k, dx, dy)
         else:
             viol, dual_part = dual_step(k, weight, count, eta, flag)
+            fpart[0] = spread(viol, own_g) + spread(dual_part, scen + own_g)
+            send(fpart.at[0], fpart.at[1], pair_sem.at[4], pair_sem.at[5], at(tm=o))
         drain_now, pending[:] = pending[:], []
         receive_dual(k)
         left = stacked(wbuf[k])
         adjoint_side(k, left)
         for n, j in enumerate(order):
             adjoint_chunk(k, j, left)
-            if k < ITERS - 1 and n == 1:
-                norm_row(k)
+            if k < ITERS - 1 and n == 0:
+                norm_middle(k)
         for copy in drain_now:
             copy.wait_send()
         if k < ITERS - 1:
-            norm_col(k)
             weight = norm_weight(k, weight, flag)
             count = jnp.where(flag > 0.5, 0.0, count)
 
     k = ITERS - 1
     dual_copy = pltpu.make_async_copy(wbuf.at[k], dual_out, out_sem.at[0])
     dual_copy.start()
-    for d in (1, 3, 2):
+    for d in near_first:
         from_r = pl.multiple_of(rem(r + rws - d, rws) * GROUP, GROUP)
         arrived(zbuf.at[pl.ds(from_r, GROUP)], z_s.at[d], z_r.at[d])
     primal_copy = pltpu.make_async_copy(zbuf, primal_out, out_sem.at[1])
     primal_copy.start()
+    arrived(fpart.at[1], pair_sem.at[4], pair_sem.at[5])
+    fixed = fpart[1] + spread(dx, 2 * scen + own_r)
     bound = jnp.zeros((GROUP, 1), jnp.float32)
     for j in order:
         part = pl.ds(j * chunk, chunk)
-        reduced = obj[:, part] - receive_adjoint(k, j)
-        bound = bound + jnp.sum(ub[:, part] * jnp.minimum(reduced, 0.0), axis=1, keepdims=True)
-    cost = dx
-    fcol[c] = tile_of([spread(viol, own_g), spread(dual_part, own_g), spread(cost, own_r), spread(bound, own_r)])
+        reduced = far[0, :, part] - receive_adjoint(k, j)
+        bound = bound + jnp.sum(far[1, :, part] * jnp.minimum(reduced, 0.0), axis=1, keepdims=True)
+    fcol[c] = fixed + spread(bound, 3 * scen + own_r)
     for d in range(1, cls):
         send(fcol.at[c], fcol.at[c], fcol_s.at[d], fcol_r.at[d], at(col=rem(c + d, cls)))
     drain_now, pending[:] = pending[:], []
+    for copy in drain_now[:-7]:
+        copy.wait_send()
     for d in range(1, cls):
         arrived(fcol.at[rem(c + cls - d, cls)], fcol_s.at[d], fcol_r.at[d])
     total = fcol[0]
     for i in range(1, cls):
         total = total + fcol[i]
-    frow[r] = total
-    for d in range(1, rws):
-        send(frow.at[r], frow.at[r], frow_s.at[d], frow_r.at[d], at(row=rem(r + d, rws)))
-    for copy in drain_now:
+    fsum[...] = total
+    for d in far_first:
+        send(fsum, frow.at[r], frow_s.at[d], frow_r.at[d], at(tm=o, row=rem(r + d, rws)))
+    for copy in drain_now[-7:]:
         copy.wait_send()
-    for d in range(1, rws):
+    dual_copy.wait()
+    primal_copy.wait()
+    for d in near_first:
         arrived(frow.at[rem(r + rws - d, rws)], frow_s.at[d], frow_r.at[d])
     total = frow[0]
     for i in range(1, rws):
         total = total + frow[i]
     con_total, var_total = float(rows * rws), float(cols * cls)
-    kkt_out[0, 0:1, :] = jnp.sqrt(total[0:1, 0:scen] / con_total + 1e-06)
-    kkt_out[0, 1:2, :] = total[2:3, 0:scen] / var_total
-    kkt_out[0, 2:3, :] = (total[1:2, 0:scen] + total[3:4, 0:scen]) / var_total
+    parts = [total[:, i * scen : (i + 1) * scen] for i in range(4)]
+    kkt_out[0, 0:1, :] = jnp.sqrt(parts[0] / con_total + 1e-06)
+    kkt_out[0, 1:2, :] = parts[2] / var_total
+    kkt_out[0, 2:3, :] = (parts[1] + parts[3]) / var_total
     drain()
-    dual_copy.wait()
-    primal_copy.wait()
 
 
 def on_device(matrix_tiles, block_map, link_tiles, demand, objective, upper_bound, restart_flag, step_index):
@@ -430,28 +447,31 @@
     scen = demand.shape[0]
     tms, rws, cls = lax.axis_size("tm"), lax.axis_size("row"), lax.axis_size("col")
     half = rows // 2
+    groups = scen // GROUP
     f32, bf16 = jnp.float32, jnp.bfloat16
     vmem = pl.BlockSpec(memory_space=pltpu.VMEM)
-    smem = pl.BlockSpec(memory_space=pltpu.SMEM)
-    anywhere = pl.BlockSpec(memory_space=pl.ANY)
+    hbm = pl.BlockSpec(memory_space=pltpu.HBM)
     V = pltpu.VMEM
     D = pltpu.SemaphoreType.DMA
     n = ITERS
     scratch = [
+        pltpu.SMEM(block_map.shape, jnp.int32), V(restart_flag.shape, jnp.int32), V(step_index.shape, jnp.int32),
+        V((GROUP, half), f32), V((2, 1, cols), f32), V((2, 1, cols), f32),
         V((rows, cols), f32), V((rows, stor), f32),
         V((rows, cols), bf16), V((rows, cols), bf16), V((rows, stor), bf16), V((rows, stor), bf16),
-        V((n, scen, cols), f32), V((n, scen, stor), f32), V((n, scen, rows), f32), V((n, cls, GROUP, half), f32),
+        V((n, scen, cols), f32), V((n, GROUP, cols), f32), V((n, scen, stor), f32), V((n, scen, rows), f32),
+        V((n, cls, GROUP, half), f32),
         V((n, scen, rows), f32), V((n, scen, cols), f32), V((n, scen, stor), f32),
-        V((n, rws, GROUP, cols), f32), V((n, rws, GROUP, stor), f32), V((scen, cols), f32),
+        V((n, rws, GROUP, cols), f32), V((n, rws, GROUP, stor), f32), V((scen, cols), f32), V((GROUP, cols), f32),
         V((GROUP, cols), f32), V((GROUP, cols), f32), V((GROUP, cols), f32),
         V((GROUP, half), f32), V((GROUP, half), f32), V((GROUP, half), f32), V((GROUP, half), f32), V((GROUP, half), f32),
-        V((n - 1, 3, 8, LANES), f32), V((n - 1, tms, 8, LANES), f32), V((n - 1, rws, 8, LANES), f32),
-        V((n - 1, cls, 8, LANES), f32), V((8, LANES), f32), V((cls, 8, LANES), f32), V((rws, 8, LANES), f32),
-        D((rows // (rows // block_map.shape[0]) + 1,)), D((2,)),
-        D(()), D(()), D((n, rws)), D((n, rws)), D((n, cls)), D((n, cls)), D((n, cls)), D((n, cls)),
+        V((n - 1, 2, 1, LANES), f32), V((n - 1, 2 * tms, 1, LANES), f32), V((n - 1, groups * rws, 1, LANES), f32),
+        V((2, 1, LANES), f32), V((cls, 1, LANES), f32), V((1, LANES), f32), V((rws, 1, LANES), f32),
+        D((block_map.shape[0] + 1,)), D((6,)), D((2,)), D((6,)),
+        D((n, rws)), D((n, rws)), D((n, cls)), D((n, cls)), D((n, cls)), D((n, cls)),
         D((n, rws)), D((n, rws)), D((n, CHUNKS, rws)), D((n, CHUNKS, rws)),
         D((n, CHUNKS, rws)), D((n, CHUNKS, rws)), D((rws,)), D((rws,)),
-        D((n - 1, tms)), D((n - 1, tms)), D((n - 1, rws)), D((n - 1, rws)), D((n - 1, cls)), D((n - 1, cls)),
+        D((n - 1, 2 * tms)), D((n - 1, 2 * tms)), D((n - 1, groups * rws)), D((n - 1, groups * rws)),
         D((cls,)), D((cls,)), D((rws,)), D((rws,)),
     ]
     return pl.pallas_call(
@@ -461,11 +481,11 @@
             jax.ShapeDtypeStruct((scen, rows), f32),
             jax.ShapeDtypeStruct((1, 3, scen), f32),
         ),
-        in_specs=[anywhere, smem, anywhere, vmem, vmem, vmem, vmem, vmem],
-        out_specs=(anywhere, anywhere, vmem),
+        in_specs=[hbm] * 8,
+        out_specs=(hbm, hbm, vmem),
         scratch_shapes=scratch,
         compiler_params=pltpu.CompilerParams(
-            collective_id=0, has_side_effects=True, vmem_limit_bytes=48 << 20
+            collective_id=0, has_side_effects=True, vmem_limit_bytes=63 << 20
         ),
         name="pdhg",
     )(

time: 121 us -> 106 us (0.88)
  Pallas kernels: 112 us -> 101 us
  local copies, waits for them, and re-layouts: 7.48 us -> 4.45 us
    pallas_call x1, Pallas kernels: 112 us -> 101 us  [on_device(): pl.pallas_call(functools.partial(kernel, (tms, rws, cls)), out_shape=(jax...]
    unnamed x16 -> x2, local copies, waits for them, and re-layouts: 6.91 us -> 3.24 us
where the time goes in v2:
time: 106 us
  Pallas kernels  101 us (95%)
  local copies, waits for them, and re-layouts  4.45 us (4%)
    pallas_call x1, Pallas kernels, on_device(): pl.pallas_call(functools.partial(kernel, (tms, rws, cls)), out_shape=(jax...  101 us
    unnamed x2, local copies, waits for them, and re-layouts  3.24 us

profile of v2, /device:TPU:1, one launch (start us, length us, event | category | flops | bytes accessed | tf_op | source)
XLA Modules:
  0.0 106.3 jit_solution(15456946031492200842)
XLA Ops:
  0.6 101.2 %pdhg.1 = (f32[32,2048]{1,0:T(8,128)}, f32[32,1024]{1,0:T(8,128)}, f32[1,3,32]{2,1,0:T(4,128)}) custom-call(f32[1024,2048]{1,0:T(8,128)} %mat.1, s32[4,8]{1,0:T(4,128)} %bmap_in.1, f32[1024,256]{1,0:T(8,128)} %link.1, f32[32,1024]{1,0:T(8,128)} %dem_in.1, f32[1,2048]{1,0:T(1,128)} %bitcast.2, f32[1,2048]{1,0:T(1,128)} %bitcast.3, s32[3,32]{1,0:T(4,128)} %flags_in.1, ...), custom_call_target="tpu_custom_call" | custom-call | tf_op jit(solution)/shard_map/pdhg/pallas_call | solution.py:477
  101.8 1.2 %copy.11 = f32[1,3,32]{2,0,1:T(1,128)} copy(f32[1,3,32]{2,1,0:T(4,128)} %get-tuple-element.5) | data formatting | bytes 768 | tf_op jit(solution)/shard_map/pdhg/pallas_call | solution.py:477
  103.0 1.7 %copy.14 = f32[32,2048]{1,0:T(8,128)} copy(f32[32,2048]{1,0:T(8,128)} %get-tuple-element.9) | data formatting | bytes 524288
  104.7 1.6 %copy.15 = f32[32,1024]{1,0:T(8,128)} copy(f32[32,1024]{1,0:T(8,128)} %get-tuple-element.10) | data formatting | bytes 262144

commit v3 on v2

--- a/solution.py
+++ b/solution.py
@@ -57,11 +57,11 @@
     kf, lf, kh, kl, lh, ll,
     ybuf, ypiece, halo, pq, qb, wbuf, pa, side, ab, sb, zbuf, zpiece,
     xs, xavg, xanc, ds, davg, danc, qx, qavg,
-    nsend, near_buf, wide_buf, fpart, fcol, fsum, frow,
-    load_sem, small_sem, out_sem, pair_sem,
+    nsend, near_buf, wide_buf, fpart, fsum, fall,
+    load_sem, small_sem, out_sem, pair_sem, hello,
     halo_s, halo_r, rsc_s, rsc_r, agc_s, agc_r,
-    side_s, side_r, rsr_s, rsr_r, agr_s, agr_r, z_s, z_r,
-    near_s, near_r, wide_s, wide_r, fcol_s, fcol_r, frow_s, frow_r,
+    side_s, side_r, rsr_s, rsr_r, agr_s, agr_r, z_sem,
+    near_s, near_r, wide_s, wide_r, fall_sem,
 ):
     tms, rws, cls = sizes
     rows, cols = kf.shape
@@ -81,7 +81,6 @@
     near_first = (0, 1, 3, 2)
     far_first = near_first[::-1]
     order = [CHUNKS - 1] + list(range(CHUNKS - 1))
-    pending = []
 
     def rem(a, n):
         return lax.rem(a, n)
@@ -89,22 +88,19 @@
     def at(tm=None, row=None, col=None):
         return {"tm": t if tm is None else tm, "row": r if row is None else row, "col": c if col is None else col}
 
-    def send(src, dst, ssem, rsem, where):
-        copy = pltpu.make_async_remote_copy(
+    def descriptor(src, dst, ssem, rsem, where):
+        return pltpu.make_async_remote_copy(
             src_ref=src, dst_ref=dst, send_sem=ssem, recv_sem=rsem, device_id=where, device_id_type=MESH
         )
-        copy.start()
-        pending.append(copy)
-
-    def arrived(dst, ssem, rsem):
-        pltpu.make_async_remote_copy(
-            src_ref=dst, dst_ref=dst, send_sem=ssem, recv_sem=rsem, device_id=at(), device_id_type=MESH
-        ).wait_recv()
-
-    def drain():
-        for copy in pending:
-            copy.wait_send()
-        pending.clear()
+
+    def send(src, dst, ssem, rsem, where):
+        descriptor(src, dst, ssem, rsem, where).start()
+
+    def arrived(whole, sem):
+        descriptor(whole, whole, sem, sem, at()).wait_recv()
+
+    def left(whole, sem):
+        descriptor(whole, whole, sem, sem, at()).wait_send()
 
     small = [
         pltpu.make_async_copy(src, dst, small_sem.at[i])
@@ -137,10 +133,9 @@
 
     behind, ahead = rem(o + tms - 1, tms), rem(o + 1, tms)
     barrier = pltpu.get_barrier_semaphore()
-    peers = [at(tm=x, row=rem(r + d, rws)) for d in (2, 1, 3) for x in (o, behind, ahead)]
-    peers += [place for _, place in wide_peers()]
-    peers += [place for _, place in near_peers()]
-    peers += [at(col=rem(g + dg, groups) * 2 + 1 - h) for dg in range(1, groups)]
+    peers = [at(row=rem(r + d, rws)) for d in (2, 1, 3)]
+    peers += [at(tm=rem(t + d, tms)) for d in range(1, tms)]
+    peers += [at(col=rem(c + d, cls)) for d in range(1, cls)]
     for peer in peers:
         pl.semaphore_signal(barrier, inc=1, device_id=peer, device_id_type=MESH)
 
@@ -165,12 +160,12 @@
             if slot % 2 != f:
                 continue
             src = pq.at[k, pl.ds(pl.multiple_of(to_g * GROUP, GROUP), GROUP), pl.ds(pl.multiple_of(hh * half, half), half)]
-            send(src, qb.at[k, slot], rsc_s.at[k, slot], rsc_r.at[k, slot], at(col=to_g * 2 + hh))
+            send(src, qb.at[k, slot], rsc_s.at[k], rsc_r.at[k], at(col=to_g * 2 + hh))
 
     def receive_rows(k):
         total = pq[k, pl.ds(own_g, GROUP), pl.ds(own_h, half)]
-        for slot, _, _, _ in col_slots():
-            arrived(qb.at[k, slot], rsc_s.at[k, slot], rsc_r.at[k, slot])
+        arrived(qb.at[k, pl.ds(1, cls - 1)], rsc_r.at[k])
+        for slot in range(1, cls):
             total = total + qb[k, slot]
         return total
 
@@ -195,7 +190,7 @@
         wbuf[k, pl.ds(own_g, GROUP), pl.ds(own_h, half)] = dual
         piece = wbuf.at[k, pl.ds(own_g, GROUP), pl.ds(own_h, half)]
         for slot, to_g, hh, _ in col_slots():
-            send(piece, piece, agc_s.at[k, slot], agc_r.at[k, slot], at(col=to_g * 2 + hh))
+            send(piece, piece, agc_s.at[k], agc_r.at[k], at(col=to_g * 2 + hh))
         davg[...] = avg
         qavg[...] = qa
         q_now = jnp.where(flg, qa, q)
@@ -207,19 +202,12 @@
         violation = jnp.sum(jnp.square(jnp.maximum(mine - q_now, 0.0)), axis=1, keepdims=True)
         return violation, jnp.sum(mine * dual, axis=1, keepdims=True)
 
-    def receive_dual(k):
-        for slot, _, hh, from_g in col_slots():
-            piece = wbuf.at[
-                k, pl.ds(pl.multiple_of(from_g * GROUP, GROUP), GROUP), pl.ds(pl.multiple_of(hh * half, half), half)
-            ]
-            arrived(piece, agc_s.at[k, slot], agc_r.at[k, slot])
-
     def adjoint_side(k, left):
         side[k] = product(left, lh[...], ll[...], NN)
         for d in range(rws):
             to_r = rem(r + d, rws)
             src = side.at[k, pl.ds(pl.multiple_of(to_r * GROUP, GROUP), GROUP)]
-            send(src, sb.at[k, d], side_s.at[k, d], side_r.at[k, d], at(tm=behind, row=to_r))
+            send(src, sb.at[k, d], side_s.at[k], side_r.at[k], at(tm=behind, row=to_r))
 
     def adjoint_chunk(k, j, left):
         part = pl.ds(j * chunk, chunk)
@@ -227,19 +215,15 @@
         for d in far_first:
             to_r = rem(r + d, rws)
             src = pa.at[k, pl.ds(pl.multiple_of(to_r * GROUP, GROUP), GROUP), part]
-            send(src, ab.at[k, d, :, part], rsr_s.at[k, j, d], rsr_r.at[k, j, d], at(tm=o, row=to_r))
+            send(src, ab.at[k, d, :, part], rsr_s.at[k], rsr_r.at[k, j], at(tm=o, row=to_r))
 
     def receive_adjoint(k, j):
         part = pl.ds(j * chunk, chunk)
-        total = None
-        for d in near_first:
-            arrived(ab.at[k, d, :, part], rsr_s.at[k, j, d], rsr_r.at[k, j, d])
-            total = ab[k, d, :, part] if total is None else total + ab[k, d, :, part]
+        arrived(ab.at[k, :, :, part], rsr_r.at[k, j])
+        total = (ab[k, 0, :, part] + ab[k, 1, :, part]) + (ab[k, 2, :, part] + ab[k, 3, :, part])
         if j == CHUNKS - 1:
-            extra = None
-            for d in range(rws):
-                arrived(sb.at[k, d], side_s.at[k, d], side_r.at[k, d])
-                extra = sb[k, d] if extra is None else extra + sb[k, d]
+            arrived(sb.at[k], side_r.at[k])
+            extra = (sb[k, 0] + sb[k, 1]) + (sb[k, 2] + sb[k, 3])
             total = jnp.concatenate([total[:, : chunk - stor], total[:, chunk - stor :] + extra], axis=1)
         return total
 
@@ -252,13 +236,13 @@
             for d in far_first:
                 send(
                     ypiece.at[k, :, part], ybuf.at[k, pl.ds(own_r, GROUP), part],
-                    agr_s.at[k, j, d], agr_r.at[k, j, d], at(tm=o, row=rem(r + d, rws)),
+                    agr_s.at[k], agr_r.at[k, j], at(tm=o, row=rem(r + d, rws)),
                 )
             if j == CHUNKS - 1:
                 for d in far_first:
                     send(
                         ypiece.at[k, :, pl.ds(edge, stor)], halo.at[k, pl.ds(own_r, GROUP)],
-                        halo_s.at[k, d], halo_r.at[k, d], at(tm=ahead, row=rem(r + d, rws)),
+                        halo_s.at[k], halo_r.at[k], at(tm=ahead, row=rem(r + d, rws)),
                     )
 
     def primal_rest(k, count, flag):
@@ -280,27 +264,19 @@
             return dist
         zpiece[...] = now
         for d in far_first:
-            send(zpiece, zbuf.at[pl.ds(own_r, GROUP)], z_s.at[d], z_r.at[d], at(tm=o, row=rem(r + d, rws)))
+            send(zpiece, zbuf.at[pl.ds(own_r, GROUP)], z_sem.at[0], z_sem.at[1], at(tm=o, row=rem(r + d, rws)))
         return jnp.sum(far[0] * now, axis=1, keepdims=True)
-
-    def receive_primal(k, j):
-        part = pl.ds(j * chunk, chunk)
-        for d in near_first:
-            piece = ybuf.at[k, pl.ds(pl.multiple_of(rem(r + rws - d, rws) * GROUP, GROUP), GROUP), part]
-            arrived(piece, agr_s.at[k, j, d], agr_r.at[k, j, d])
 
     def apply_chunks(k):
         acc = None
         for j in order:
-            receive_primal(k, j)
             part = pl.ds(j * chunk, chunk)
+            arrived(ybuf.at[k, :, part], agr_r.at[k, j])
             left = stacked(ybuf[k, :, part])
             if j != order[-1]:
                 term = product(left, kh[:, part], kl[:, part], NT)
                 if j == CHUNKS - 1:
-                    for d in range(rws):
-                        from_r = pl.multiple_of(rem(r + rws - d, rws) * GROUP, GROUP)
-                        arrived(halo.at[k, pl.ds(from_r, GROUP)], halo_s.at[k, d], halo_r.at[k, d])
+                    arrived(halo.at[k], halo_r.at[k])
                     pq[k] = term + product(stacked(halo[k]), lh[...], ll[...], NT)
                 else:
                     pq[k] = pq[k] + term
@@ -314,21 +290,21 @@
     def norm_start(k, dx, dy):
         nsend[k, 0] = spread(dx, own_r) + spread(dy, scen + own_g)
         for slot, place in near_peers():
-            send(nsend.at[k, 0], near_buf.at[k, slot], near_s.at[k, slot], near_r.at[k, slot], place)
+            send(nsend.at[k, 0], near_buf.at[k, slot], near_s.at[k], near_r.at[k], place)
 
     def norm_middle(k):
         total = nsend[k, 0]
+        arrived(near_buf.at[k, pl.ds(1, 2 * tms - 1)], near_r.at[k])
         for slot, _ in near_peers():
-            arrived(near_buf.at[k, slot], near_s.at[k, slot], near_r.at[k, slot])
             total = total + near_buf[k, slot]
         nsend[k, 1] = total
         for slot, place in wide_peers():
-            send(nsend.at[k, 1], wide_buf.at[k, slot], wide_s.at[k, slot], wide_r.at[k, slot], place)
+            send(nsend.at[k, 1], wide_buf.at[k, slot], wide_s.at[k], wide_r.at[k], place)
 
     def norm_weight(k, weight, flag):
         total = nsend[k, 1]
+        arrived(wide_buf.at[k, pl.ds(1, groups * rws - 1)], wide_r.at[k])
         for slot, _ in wide_peers():
-            arrived(wide_buf.at[k, slot], wide_s.at[k, slot], wide_r.at[k, slot])
             total = total + wide_buf[k, slot]
         dx, dy = total[:, 0:scen], total[:, scen : 2 * scen]
         candidate = jnp.sqrt((dy + 1e-06) / (dx + 1e-06))
@@ -353,17 +329,20 @@
             pl.semaphore_wait(barrier, len(peers))
             send(ybuf.at[0, :, pl.ds(edge, stor)], halo.at[0], pair_sem.at[0], pair_sem.at[1], at(tm=rem(t + 1, tms)))
             send(costs, far, pair_sem.at[2], pair_sem.at[3], at(tm=o))
+            for x in (behind, ahead):
+                pl.semaphore_signal(hello, inc=1, device_id=at(tm=x), device_id_type=MESH)
     loads[-1].wait()
     high, low = halves(lf[...])
     lh[...] = high
     ll[...] = low
-    arrived(halo.at[0], pair_sem.at[0], pair_sem.at[1])
+    arrived(halo.at[0], pair_sem.at[1])
     left0 = stacked(halo[0])
     for f in (1, 0):
         some = pl.ds(pl.multiple_of((h if f == 0 else 1 - h) * half, half), half)
         pq[0, :, some] = pq[0, :, some] + product(left0, lh[some, :], ll[some, :], NT)
         send_rows_half(0, f)
-    arrived(far, pair_sem.at[2], pair_sem.at[3])
+    arrived(far, pair_sem.at[3])
+    pl.semaphore_wait(hello, 2)
     ypiece[0] = jnp.clip(-column(eta, own_r, GROUP) * far[0], 0.0, far[1])
     dx = primal_rest(0, count, flag)
 
@@ -381,16 +360,13 @@
             viol, dual_part = dual_step(k, weight, count, eta, flag)
             fpart[0] = spread(viol, own_g) + spread(dual_part, scen + own_g)
             send(fpart.at[0], fpart.at[1], pair_sem.at[4], pair_sem.at[5], at(tm=o))
-        drain_now, pending[:] = pending[:], []
-        receive_dual(k)
-        left = stacked(wbuf[k])
-        adjoint_side(k, left)
+        arrived(qb.at[k, pl.ds(1, cls - 1)], agc_r.at[k])
+        dual_parts = stacked(wbuf[k])
+        adjoint_side(k, dual_parts)
         for n, j in enumerate(order):
-            adjoint_chunk(k, j, left)
+            adjoint_chunk(k, j, dual_parts)
             if k < ITERS - 1 and n == 0:
                 norm_middle(k)
-        for copy in drain_now:
-            copy.wait_send()
         if k < ITERS - 1:
             weight = norm_weight(k, weight, flag)
             count = jnp.where(flag > 0.5, 0.0, count)
@@ -398,47 +374,48 @@
     k = ITERS - 1
     dual_copy = pltpu.make_async_copy(wbuf.at[k], dual_out, out_sem.at[0])
     dual_copy.start()
-    for d in near_first:
-        from_r = pl.multiple_of(rem(r + rws - d, rws) * GROUP, GROUP)
-        arrived(zbuf.at[pl.ds(from_r, GROUP)], z_s.at[d], z_r.at[d])
+    arrived(zbuf, z_sem.at[1])
     primal_copy = pltpu.make_async_copy(zbuf, primal_out, out_sem.at[1])
     primal_copy.start()
-    arrived(fpart.at[1], pair_sem.at[4], pair_sem.at[5])
+    arrived(fpart.at[1], pair_sem.at[5])
     fixed = fpart[1] + spread(dx, 2 * scen + own_r)
     bound = jnp.zeros((GROUP, 1), jnp.float32)
     for j in order:
         part = pl.ds(j * chunk, chunk)
         reduced = far[0, :, part] - receive_adjoint(k, j)
         bound = bound + jnp.sum(far[1, :, part] * jnp.minimum(reduced, 0.0), axis=1, keepdims=True)
-    fcol[c] = fixed + spread(bound, 3 * scen + own_r)
-    for d in range(1, cls):
-        send(fcol.at[c], fcol.at[c], fcol_s.at[d], fcol_r.at[d], at(col=rem(c + d, cls)))
-    drain_now, pending[:] = pending[:], []
-    for copy in drain_now[:-7]:
-        copy.wait_send()
-    for d in range(1, cls):
-        arrived(fcol.at[rem(c + cls - d, cls)], fcol_s.at[d], fcol_r.at[d])
-    total = fcol[0]
-    for i in range(1, cls):
-        total = total + fcol[i]
-    fsum[...] = total
-    for d in far_first:
-        send(fsum, frow.at[r], frow_s.at[d], frow_r.at[d], at(tm=o, row=rem(r + d, rws)))
-    for copy in drain_now[-7:]:
-        copy.wait_send()
+    fsum[...] = fixed + spread(bound, 3 * scen + own_r)
+    for dr in far_first:
+        for dc in (4, 3, 5, 2, 6, 1, 7, 0):
+            place = at(tm=o, row=rem(r + dr, rws), col=rem(c + dc, cls))
+            send(fsum, fall.at[r * cls + c], fall_sem.at[0], fall_sem.at[1], place)
+    left(halo.at[0], pair_sem.at[0])
+    left(costs, pair_sem.at[2])
+    left(fpart.at[0], pair_sem.at[4])
+    left(zbuf, z_sem.at[0])
+    for k in range(ITERS):
+        left(qb.at[k, pl.ds(1, cls - 1)], rsc_s.at[k])
+        left(qb.at[k, pl.ds(1, cls - 1)], agc_s.at[k])
+        left(side.at[k], side_s.at[k])
+        left(pa.at[k], rsr_s.at[k])
+        if k > 0:
+            left(ybuf.at[k], agr_s.at[k])
+            left(halo.at[k], halo_s.at[k])
+        if k < ITERS - 1:
+            left(near_buf.at[k, pl.ds(1, 2 * tms - 1)], near_s.at[k])
+            left(wide_buf.at[k, pl.ds(1, groups * rws - 1)], wide_s.at[k])
+    left(fall, fall_sem.at[0])
     dual_copy.wait()
     primal_copy.wait()
-    for d in near_first:
-        arrived(frow.at[rem(r + rws - d, rws)], frow_s.at[d], frow_r.at[d])
-    total = frow[0]
-    for i in range(1, rws):
-        total = total + frow[i]
+    arrived(fall, fall_sem.at[1])
+    total = fall[0]
+    for i in range(1, rws * cls):
+        total = total + fall[i]
     con_total, var_total = float(rows * rws), float(cols * cls)
     parts = [total[:, i * scen : (i + 1) * scen] for i in range(4)]
     kkt_out[0, 0:1, :] = jnp.sqrt(parts[0] / con_total + 1e-06)
     kkt_out[0, 1:2, :] = parts[2] / var_total
     kkt_out[0, 2:3, :] = (parts[1] + parts[3]) / var_total
-    drain()
 
 
 def on_device(matrix_tiles, block_map, link_tiles, demand, objective, upper_bound, restart_flag, step_index):
@@ -466,13 +443,11 @@
         V((GROUP, cols), f32), V((GROUP, cols), f32), V((GROUP, cols), f32),
         V((GROUP, half), f32), V((GROUP, half), f32), V((GROUP, half), f32), V((GROUP, half), f32), V((GROUP, half), f32),
         V((n - 1, 2, 1, LANES), f32), V((n - 1, 2 * tms, 1, LANES), f32), V((n - 1, groups * rws, 1, LANES), f32),
-        V((2, 1, LANES), f32), V((cls, 1, LANES), f32), V((1, LANES), f32), V((rws, 1, LANES), f32),
-        D((block_map.shape[0] + 1,)), D((6,)), D((2,)), D((6,)),
-        D((n, rws)), D((n, rws)), D((n, cls)), D((n, cls)), D((n, cls)), D((n, cls)),
-        D((n, rws)), D((n, rws)), D((n, CHUNKS, rws)), D((n, CHUNKS, rws)),
-        D((n, CHUNKS, rws)), D((n, CHUNKS, rws)), D((rws,)), D((rws,)),
-        D((n - 1, 2 * tms)), D((n - 1, 2 * tms)), D((n - 1, groups * rws)), D((n - 1, groups * rws)),
-        D((cls,)), D((cls,)), D((rws,)), D((rws,)),
+        V((2, 1, LANES), f32), V((1, LANES), f32), V((rws * cls, 1, LANES), f32),
+        D((block_map.shape[0] + 1,)), D((6,)), D((2,)), D((6,)), pltpu.SemaphoreType.REGULAR,
+        D((n,)), D((n,)), D((n,)), D((n,)), D((n,)), D((n,)),
+        D((n,)), D((n,)), D((n,)), D((n, CHUNKS)), D((n,)), D((n, CHUNKS)), D((2,)),
+        D((n - 1,)), D((n - 1,)), D((n - 1,)), D((n - 1,)), D((2,)),
     ]
     return pl.pallas_call(
         functools.partial(kernel, (tms, rws, cls)),
@@ -485,13 +460,16 @@
         out_specs=(hbm, hbm, vmem),
         scratch_shapes=scratch,
         compiler_params=pltpu.CompilerParams(
-            collective_id=0, has_side_effects=True, vmem_limit_bytes=63 << 20
+            collective_id=0, has_side_effects=True, vmem_limit_bytes=48 << 20
         ),
         name="pdhg",
-    )(
-        matrix_tiles, block_map, link_tiles, demand, objective.reshape(1, cols), upper_bound.reshape(1, cols),
-        restart_flag, step_index,
-    )
+    )(*(
+        pltpu.with_memory_space_constraint(x, pltpu.HBM)
+        for x in (
+            matrix_tiles, block_map, link_tiles, demand, objective.reshape(1, cols), upper_bound.reshape(1, cols),
+            restart_flag, step_index,
+        )
+    ))
 
 
 def solution(mesh):

time: 106 us -> 98.4 us (0.928)
  Pallas kernels: 101 us -> 95.8 us
  local copies, waits for them, and re-layouts: 4.45 us -> 1.92 us
    pallas_call x1, Pallas kernels: 101 us -> 95.8 us  [on_device(): pl.pallas_call(functools.partial(kernel, (tms, rws, cls)), out_shape=(jax...]
    unnamed x2, local copies, waits for them, and re-layouts: 3.24 us -> 1.36 us
where the time goes in v3:
time: 98.4 us; the launch traced here: 98.3 us
  Pallas kernels  95.8 us (97%)
  local copies, waits for them, and re-layouts  1.92 us (2%)
    pallas_call x1, Pallas kernels, on_device(): pl.pallas_call(functools.partial(kernel, (tms, rws, cls)), out_shape=(jax...  95.8 us

profile of v3, /device:TPU:1, one launch (start us, length us, event | category | flops | bytes accessed | tf_op | source)
XLA Modules:
  0.0 98.3 jit_solution(7686248172490549883)
XLA Ops:
  0.6 95.8 %pdhg.1 = (f32[32,2048]{1,0:T(8,128)S(1)}, f32[32,1024]{1,0:T(8,128)S(1)}, f32[1,3,32]{2,1,0:T(4,128)S(1)}) custom-call(f32[1024,2048]{1,0:T(8,128)} %mat.1, s32[4,8]{1,0:T(4,128)} %bmap_in.1, f32[1024,256]{1,0:T(8,128)} %link.1, f32[32,1024]{1,0:T(8,128)} %dem_in.1, f32[1,2048]{1,0:T(1,128)} %bitcast.2, f32[1,2048]{1,0:T(1,128)} %bitcast.3, ...), custom_call_target="tpu_custom_call" | custom-call | tf_op jit(solution)/shard_map/pdhg/pallas_call | solution.py:452
  96.4 0.6 copy.11
  97.0 0.7 copy.14
  97.7 0.7 copy.15

commit v4 on v3

--- a/solution.py
+++ b/solution.py
@@ -8,7 +8,7 @@
 from jax.sharding import PartitionSpec as P
 
 ITERS = 3
-CHUNKS = 4
+CHUNKS = ((0, 256), (1792, 256), (256, 512), (768, 512), (1280, 512))
 LANES = 128
 GROUP = 8
 MESH = pl.DeviceIdType.MESH
@@ -55,12 +55,12 @@
     primal_out, dual_out, kkt_out,
     bmap, flags, steps, dem, costs, far,
     kf, lf, kh, kl, lh, ll,
-    ybuf, ypiece, halo, pq, qb, wbuf, pa, side, ab, sb, zbuf, zpiece,
+    ybuf, gsum, gbuf, halo, pq, qb, wbuf, pa, side, ab, sb, zbuf,
     xs, xavg, xanc, ds, davg, danc, qx, qavg,
-    nsend, near_buf, wide_buf, fpart, fsum, fall,
+    near_buf, wide_buf, fpart, fsum, fall,
     load_sem, small_sem, out_sem, pair_sem, hello,
     halo_s, halo_r, rsc_s, rsc_r, agc_s, agc_r,
-    side_s, side_r, rsr_s, rsr_r, agr_s, agr_r, z_sem,
+    side_s, side_r, rsr_s, rsr_r, agr_s, agr_r,
     near_s, near_r, wide_s, wide_r, fall_sem,
 ):
     tms, rws, cls = sizes
@@ -68,7 +68,6 @@
     stor = lf.shape[1]
     edge = cols - stor
     scen = ybuf.shape[1]
-    chunk = cols // CHUNKS
     half = rows // 2
     groups = scen // GROUP
     blk = rows // bmap.shape[0]
@@ -80,7 +79,7 @@
     own_h = pl.multiple_of(h * half, half)
     near_first = (0, 1, 3, 2)
     far_first = near_first[::-1]
-    order = [CHUNKS - 1] + list(range(CHUNKS - 1))
+    final = len(CHUNKS) - 1
 
     def rem(a, n):
         return lax.rem(a, n)
@@ -123,13 +122,13 @@
         for dt in range(tms):
             for f in range(2):
                 if dt or f:
-                    yield dt * 2 + f, at(tm=rem(t + dt, tms), col=g * 2 + (1 - h if f else h))
+                    yield at(tm=rem(t + dt, tms), col=g * 2 + (1 - h if f else h))
 
     def wide_peers():
         for dr in (2, 1, 3, 0):
             for dg in range(groups):
                 if dr or dg:
-                    yield dr * groups + dg, at(row=rem(r + dr, rws), col=rem(g + dg, groups) * 2 + h)
+                    yield at(row=rem(r + dr, rws), col=rem(g + dg, groups) * 2 + h)
 
     behind, ahead = rem(o + tms - 1, tms), rem(o + 1, tms)
     barrier = pltpu.get_barrier_semaphore()
@@ -210,7 +209,7 @@
             send(src, sb.at[k, d], side_s.at[k], side_r.at[k], at(tm=behind, row=to_r))
 
     def adjoint_chunk(k, j, left):
-        part = pl.ds(j * chunk, chunk)
+        part = pl.ds(*CHUNKS[j])
         pa[k, :, part] = product(left, kh[:, part], kl[:, part], NN)
         for d in far_first:
             to_r = rem(r + d, rws)
@@ -218,68 +217,62 @@
             send(src, ab.at[k, d, :, part], rsr_s.at[k], rsr_r.at[k, j], at(tm=o, row=to_r))
 
     def receive_adjoint(k, j):
-        part = pl.ds(j * chunk, chunk)
+        part = pl.ds(*CHUNKS[j])
         arrived(ab.at[k, :, :, part], rsr_r.at[k, j])
         total = (ab[k, 0, :, part] + ab[k, 1, :, part]) + (ab[k, 2, :, part] + ab[k, 3, :, part])
-        if j == CHUNKS - 1:
+        if CHUNKS[j][0] == edge:
             arrived(sb.at[k], side_r.at[k])
             extra = (sb[k, 0] + sb[k, 1]) + (sb[k, 2] + sb[k, 3])
-            total = jnp.concatenate([total[:, : chunk - stor], total[:, chunk - stor :] + extra], axis=1)
+            total = total + extra
         return total
 
-    def primal_steps(k, weight, eta):
-        tau = column(eta / weight, own_r, GROUP)
-        for j in order:
-            part = pl.ds(j * chunk, chunk)
-            reduced = far[0, :, part] - receive_adjoint(k - 1, j)
-            ypiece[k, :, part] = jnp.clip(xs[:, part] - tau * reduced, 0.0, far[1, :, part])
+    def adjoint_sums(k):
+        for j in range(len(CHUNKS)):
+            part = pl.ds(*CHUNKS[j])
+            gsum[k, :, part] = receive_adjoint(k, j)
             for d in far_first:
                 send(
-                    ypiece.at[k, :, part], ybuf.at[k, pl.ds(own_r, GROUP), part],
+                    gsum.at[k, :, part], gbuf.at[k, pl.ds(own_r, GROUP), part],
                     agr_s.at[k], agr_r.at[k, j], at(tm=o, row=rem(r + d, rws)),
                 )
-            if j == CHUNKS - 1:
-                for d in far_first:
-                    send(
-                        ypiece.at[k, :, pl.ds(edge, stor)], halo.at[k, pl.ds(own_r, GROUP)],
-                        halo_s.at[k], halo_r.at[k], at(tm=ahead, row=rem(r + d, rws)),
-                    )
 
     def primal_rest(k, count, flag):
-        cnt = column(count, own_r, GROUP)
-        flg = column(flag, own_r, GROUP) > 0.5
-        nxt = ypiece[k]
-        if k == 0:
-            avg = nxt
-            anchor = jnp.zeros_like(nxt)
-        else:
-            avg = xavg[...] + (nxt - xavg[...]) / cnt
-            anchor = xanc[...]
-        now = jnp.where(flg, avg, nxt)
-        xs[...] = now
-        xavg[...] = avg
-        dist = jnp.sum(jnp.square(avg - anchor), axis=1, keepdims=True)
-        xanc[...] = jnp.where(flg, avg, anchor)
-        if k < ITERS - 1:
-            return dist
-        zpiece[...] = now
-        for d in far_first:
-            send(zpiece, zbuf.at[pl.ds(own_r, GROUP)], z_sem.at[0], z_sem.at[1], at(tm=o, row=rem(r + d, rws)))
-        return jnp.sum(far[0] * now, axis=1, keepdims=True)
-
-    def apply_chunks(k):
-        acc = None
-        for j in order:
-            part = pl.ds(j * chunk, chunk)
-            arrived(ybuf.at[k, :, part], agr_r.at[k, j])
-            left = stacked(ybuf[k, :, part])
-            if j != order[-1]:
+        cnt = column(count, 0, scen)
+        flg = column(flag, 0, scen) > 0.5
+        mine = pl.ds(own_r, GROUP)
+        for first, size in CHUNKS:
+            part = pl.ds(first, size)
+            nxt = ybuf[k, :, part]
+            avg = nxt if k == 0 else xavg[:, part] + (nxt - xavg[:, part]) / cnt
+            xavg[:, part] = avg
+            now = jnp.where(flg, avg, nxt)
+            if k < ITERS - 1:
+                xs[:, part] = now
+            else:
+                zbuf[:, part] = now
+        if k == ITERS - 1:
+            return jnp.sum(costs[0] * zbuf[mine, :], axis=1, keepdims=True)
+        avg = xavg[mine, :]
+        anchor = jnp.zeros_like(avg) if k == 0 else xanc[...]
+        xanc[...] = jnp.where(column(flag, own_r, GROUP) > 0.5, avg, anchor)
+        return jnp.sum(jnp.square(avg - anchor), axis=1, keepdims=True)
+
+    def apply_chunks(k, tau):
+        for j in range(len(CHUNKS)):
+            part = pl.ds(*CHUNKS[j])
+            arrived(gbuf.at[k - 1, :, part], agr_r.at[k - 1, j])
+            reduced = costs[0, :, part] - gbuf[k - 1, :, part]
+            nxt = jnp.clip(xs[:, part] - tau * reduced, 0.0, costs[1, :, part])
+            ybuf[k, :, part] = nxt
+            left = stacked(nxt)
+            if CHUNKS[j][0] == edge:
+                send(ybuf.at[k, :, part], halo.at[k], halo_s.at[k], halo_r.at[k], at(tm=rem(t + 1, tms)))
+            if j != final:
                 term = product(left, kh[:, part], kl[:, part], NT)
-                if j == CHUNKS - 1:
+                if j == final - 1:
                     arrived(halo.at[k], halo_r.at[k])
-                    pq[k] = term + product(stacked(halo[k]), lh[...], ll[...], NT)
-                else:
-                    pq[k] = pq[k] + term
+                    term = term + product(stacked(halo[k]), lh[...], ll[...], NT)
+                pq[k] = term if j == 0 else pq[k] + term
             else:
                 for f in (1, 0):
                     hh = pl.multiple_of((h if f == 0 else 1 - h) * half, half)
@@ -288,24 +281,26 @@
                     send_rows_half(k, f)
 
     def norm_start(k, dx, dy):
-        nsend[k, 0] = spread(dx, own_r) + spread(dy, scen + own_g)
-        for slot, place in near_peers():
-            send(nsend.at[k, 0], near_buf.at[k, slot], near_s.at[k], near_r.at[k], place)
+        place = t * 2 + h
+        near_buf[k, place] = spread(dx, own_r) + spread(dy, scen + own_g)
+        for peer in near_peers():
+            send(near_buf.at[k, place], near_buf.at[k, place], near_s.at[k], near_r.at[k], peer)
 
     def norm_middle(k):
-        total = nsend[k, 0]
         arrived(near_buf.at[k, pl.ds(1, 2 * tms - 1)], near_r.at[k])
-        for slot, _ in near_peers():
-            total = total + near_buf[k, slot]
-        nsend[k, 1] = total
-        for slot, place in wide_peers():
-            send(nsend.at[k, 1], wide_buf.at[k, slot], wide_s.at[k], wide_r.at[k], place)
+        total = near_buf[k, 0]
+        for i in range(1, 2 * tms):
+            total = total + near_buf[k, i]
+        place = r * groups + g
+        wide_buf[k, place] = total
+        for peer in wide_peers():
+            send(wide_buf.at[k, place], wide_buf.at[k, place], wide_s.at[k], wide_r.at[k], peer)
 
     def norm_weight(k, weight, flag):
-        total = nsend[k, 1]
         arrived(wide_buf.at[k, pl.ds(1, groups * rws - 1)], wide_r.at[k])
-        for slot, _ in wide_peers():
-            total = total + wide_buf[k, slot]
+        total = wide_buf[k, 0]
+        for i in range(1, groups * rws):
+            total = total + wide_buf[k, i]
         dx, dy = total[:, 0:scen], total[:, scen : 2 * scen]
         candidate = jnp.sqrt((dy + 1e-06) / (dx + 1e-06))
         return jnp.where(flag > 0.5, jnp.sqrt(weight * candidate), weight)
@@ -329,8 +324,7 @@
             pl.semaphore_wait(barrier, len(peers))
             send(ybuf.at[0, :, pl.ds(edge, stor)], halo.at[0], pair_sem.at[0], pair_sem.at[1], at(tm=rem(t + 1, tms)))
             send(costs, far, pair_sem.at[2], pair_sem.at[3], at(tm=o))
-            for x in (behind, ahead):
-                pl.semaphore_signal(hello, inc=1, device_id=at(tm=x), device_id_type=MESH)
+            pl.semaphore_signal(hello, inc=1, device_id=at(tm=ahead), device_id_type=MESH)
     loads[-1].wait()
     high, low = halves(lf[...])
     lh[...] = high
@@ -342,49 +336,48 @@
         pq[0, :, some] = pq[0, :, some] + product(left0, lh[some, :], ll[some, :], NT)
         send_rows_half(0, f)
     arrived(far, pair_sem.at[3])
-    pl.semaphore_wait(hello, 2)
-    ypiece[0] = jnp.clip(-column(eta, own_r, GROUP) * far[0], 0.0, far[1])
+    pl.semaphore_wait(hello, 1)
     dx = primal_rest(0, count, flag)
 
     for k in range(ITERS):
         if k > 0:
             eta, flag = plan(k)
             count = count + 1.0
-            primal_steps(k, weight, eta)
+            apply_chunks(k, column(eta / weight, 0, scen))
             dx = primal_rest(k, count, flag)
-            apply_chunks(k)
+            if k == ITERS - 1:
+                primal_copy = pltpu.make_async_copy(zbuf, primal_out, out_sem.at[1])
+                primal_copy.start()
         if k < ITERS - 1:
             dy = dual_step(k, weight, count, eta, flag)
             norm_start(k, dx, dy)
         else:
             viol, dual_part = dual_step(k, weight, count, eta, flag)
-            fpart[0] = spread(viol, own_g) + spread(dual_part, scen + own_g)
+            fpart[0] = spread(viol, own_g) + spread(dual_part, scen + own_g) + spread(dx, 2 * scen + own_r)
             send(fpart.at[0], fpart.at[1], pair_sem.at[4], pair_sem.at[5], at(tm=o))
         arrived(qb.at[k, pl.ds(1, cls - 1)], agc_r.at[k])
         dual_parts = stacked(wbuf[k])
-        adjoint_side(k, dual_parts)
-        for n, j in enumerate(order):
+        for j in range(len(CHUNKS)):
             adjoint_chunk(k, j, dual_parts)
-            if k < ITERS - 1 and n == 0:
-                norm_middle(k)
+            if j == 0:
+                adjoint_side(k, dual_parts)
+                if k < ITERS - 1:
+                    norm_middle(k)
         if k < ITERS - 1:
+            adjoint_sums(k)
             weight = norm_weight(k, weight, flag)
             count = jnp.where(flag > 0.5, 0.0, count)
 
     k = ITERS - 1
     dual_copy = pltpu.make_async_copy(wbuf.at[k], dual_out, out_sem.at[0])
     dual_copy.start()
-    arrived(zbuf, z_sem.at[1])
-    primal_copy = pltpu.make_async_copy(zbuf, primal_out, out_sem.at[1])
-    primal_copy.start()
     arrived(fpart.at[1], pair_sem.at[5])
-    fixed = fpart[1] + spread(dx, 2 * scen + own_r)
     bound = jnp.zeros((GROUP, 1), jnp.float32)
-    for j in order:
-        part = pl.ds(j * chunk, chunk)
+    for j in range(len(CHUNKS)):
+        part = pl.ds(*CHUNKS[j])
         reduced = far[0, :, part] - receive_adjoint(k, j)
         bound = bound + jnp.sum(far[1, :, part] * jnp.minimum(reduced, 0.0), axis=1, keepdims=True)
-    fsum[...] = fixed + spread(bound, 3 * scen + own_r)
+    fsum[...] = fpart[1] + spread(bound, 3 * scen + own_r)
     for dr in far_first:
         for dc in (4, 3, 5, 2, 6, 1, 7, 0):
             place = at(tm=o, row=rem(r + dr, rws), col=rem(c + dc, cls))
@@ -392,14 +385,13 @@
     left(halo.at[0], pair_sem.at[0])
     left(costs, pair_sem.at[2])
     left(fpart.at[0], pair_sem.at[4])
-    left(zbuf, z_sem.at[0])
     for k in range(ITERS):
         left(qb.at[k, pl.ds(1, cls - 1)], rsc_s.at[k])
         left(qb.at[k, pl.ds(1, cls - 1)], agc_s.at[k])
         left(side.at[k], side_s.at[k])
         left(pa.at[k], rsr_s.at[k])
         if k > 0:
-            left(ybuf.at[k], agr_s.at[k])
+            left(gbuf.at[k - 1], agr_s.at[k - 1])
             left(halo.at[k], halo_s.at[k])
         if k < ITERS - 1:
             left(near_buf.at[k, pl.ds(1, 2 * tms - 1)], near_s.at[k])
@@ -436,17 +428,17 @@
         V((GROUP, half), f32), V((2, 1, cols), f32), V((2, 1, cols), f32),
         V((rows, cols), f32), V((rows, stor), f32),
         V((rows, cols), bf16), V((rows, cols), bf16), V((rows, stor), bf16), V((rows, stor), bf16),
-        V((n, scen, cols), f32), V((n, GROUP, cols), f32), V((n, scen, stor), f32), V((n, scen, rows), f32),
+        V((n, scen, cols), f32), V((n - 1, GROUP, cols), f32), V((n - 1, scen, cols), f32), V((n, scen, stor), f32), V((n, scen, rows), f32),
         V((n, cls, GROUP, half), f32),
         V((n, scen, rows), f32), V((n, scen, cols), f32), V((n, scen, stor), f32),
-        V((n, rws, GROUP, cols), f32), V((n, rws, GROUP, stor), f32), V((scen, cols), f32), V((GROUP, cols), f32),
-        V((GROUP, cols), f32), V((GROUP, cols), f32), V((GROUP, cols), f32),
+        V((n, rws, GROUP, cols), f32), V((n, rws, GROUP, stor), f32), V((scen, cols), f32),
+        V((scen, cols), f32), V((scen, cols), f32), V((GROUP, cols), f32),
         V((GROUP, half), f32), V((GROUP, half), f32), V((GROUP, half), f32), V((GROUP, half), f32), V((GROUP, half), f32),
-        V((n - 1, 2, 1, LANES), f32), V((n - 1, 2 * tms, 1, LANES), f32), V((n - 1, groups * rws, 1, LANES), f32),
+        V((n - 1, 2 * tms, 1, LANES), f32), V((n - 1, groups * rws, 1, LANES), f32),
         V((2, 1, LANES), f32), V((1, LANES), f32), V((rws * cls, 1, LANES), f32),
         D((block_map.shape[0] + 1,)), D((6,)), D((2,)), D((6,)), pltpu.SemaphoreType.REGULAR,
         D((n,)), D((n,)), D((n,)), D((n,)), D((n,)), D((n,)),
-        D((n,)), D((n,)), D((n,)), D((n, CHUNKS)), D((n,)), D((n, CHUNKS)), D((2,)),
+        D((n,)), D((n,)), D((n,)), D((n, len(CHUNKS))), D((n - 1,)), D((n - 1, len(CHUNKS))),
         D((n - 1,)), D((n - 1,)), D((n - 1,)), D((n - 1,)), D((2,)),
     ]
     return pl.pallas_call(

time: 98.4 us -> 95 us (0.965)
  Pallas kernels: 95.8 us -> 92.4 us
    pallas_call x1, Pallas kernels: 95.8 us -> 92.4 us  [on_device(): pl.pallas_call(functools.partial(kernel, (tms, rws, cls)), out_shape=(jax...]
where the time goes in v4:
time: 95 us; the launch traced here: 94.9 us
  Pallas kernels  92.4 us (97%)
  local copies, waits for them, and re-layouts  1.92 us (2%)
    pallas_call x1, Pallas kernels, on_device(): pl.pallas_call(functools.partial(kernel, (tms, rws, cls)), out_shape=(jax...  92.4 us

profile of v4, /device:TPU:1, one launch (start us, length us, event | category | flops | bytes accessed | tf_op | source)
XLA Modules:
  0.0 94.9 jit_solution(18347154355463531720)
XLA Ops:
  0.6 92.4 %pdhg.1 = (f32[32,2048]{1,0:T(8,128)S(1)}, f32[32,1024]{1,0:T(8,128)S(1)}, f32[1,3,32]{2,1,0:T(4,128)S(1)}) custom-call(f32[1024,2048]{1,0:T(8,128)} %mat.1, s32[4,8]{1,0:T(4,128)} %bmap_in.1, f32[1024,256]{1,0:T(8,128)} %link.1, f32[32,1024]{1,0:T(8,128)} %dem_in.1, f32[1,2048]{1,0:T(1,128)} %bitcast.2, f32[1,2048]{1,0:T(1,128)} %bitcast.3, ...), custom_call_target="tpu_custom_call" | custom-call | tf_op jit(solution)/shard_map/pdhg/pallas_call | solution.py:444
  93.0 0.6 copy.11
  93.6 0.7 copy.14
  94.3 0.7 copy.15

commit v5 on v4

--- a/solution.py
+++ b/solution.py
@@ -55,11 +55,11 @@
     primal_out, dual_out, kkt_out,
     bmap, flags, steps, dem, costs, far,
     kf, lf, kh, kl, lh, ll,
-    ybuf, gsum, gbuf, halo, pq, qb, wbuf, pa, side, ab, sb, zbuf,
+    ybuf, gsum, gbuf, halo, pq, sib, ysum, wbuf, pa, side, ab, sb, zbuf,
     xs, xavg, xanc, ds, davg, danc, qx, qavg,
     near_buf, wide_buf, fpart, fsum, fall,
     load_sem, small_sem, out_sem, pair_sem, hello,
-    halo_s, halo_r, rsc_s, rsc_r, agc_s, agc_r,
+    halo_s, halo_r, sib_s, sib_r, y_s, y_r, dual_s, dual_r,
     side_s, side_r, rsr_s, rsr_r, agr_s, agr_r,
     near_s, near_r, wide_s, wide_r, fall_sem,
 ):
@@ -75,8 +75,8 @@
     g, h = lax.div(c, 2), lax.rem(c, 2)
     o = lax.rem(t + tms // 2, tms)
     own_r = pl.multiple_of(r * GROUP, GROUP)
-    own_g = pl.multiple_of(g * GROUP, GROUP)
-    own_h = pl.multiple_of(h * half, half)
+    own_h = pl.ds(pl.multiple_of(h * half, half), half)
+    other_h = pl.ds(pl.multiple_of((1 - h) * half, half), half)
     near_first = (0, 1, 3, 2)
     far_first = near_first[::-1]
     final = len(CHUNKS) - 1
@@ -106,7 +106,7 @@
         for i, (src, dst) in enumerate(
             (
                 (steps_in, steps), (obj_in, costs.at[0]), (ub_in, costs.at[1]), (bmap_in, bmap), (flags_in, flags),
-                (dem_in.at[pl.ds(own_g, GROUP), pl.ds(own_h, half)], dem),
+                (dem_in.at[:, own_h], dem),
             )
         )
     ]
@@ -146,33 +146,22 @@
         flag = flags[k : k + 1, :].astype(jnp.float32)
         return eta, flag
 
-    def col_slots():
-        for f in (1, 0):
-            for dg in range(groups):
-                if f == 0 and dg == 0:
-                    continue
-                hh = h if f == 0 else 1 - h
-                yield dg * 2 + f, rem(g + dg, groups), hh, rem(g + groups - dg, groups)
-
-    def send_rows_half(k, f):
-        for slot, to_g, hh, _ in col_slots():
-            if slot % 2 != f:
-                continue
-            src = pq.at[k, pl.ds(pl.multiple_of(to_g * GROUP, GROUP), GROUP), pl.ds(pl.multiple_of(hh * half, half), half)]
-            send(src, qb.at[k, slot], rsc_s.at[k], rsc_r.at[k], at(col=to_g * 2 + hh))
-
-    def receive_rows(k):
-        total = pq[k, pl.ds(own_g, GROUP), pl.ds(own_h, half)]
-        arrived(qb.at[k, pl.ds(1, cls - 1)], rsc_r.at[k])
-        for slot in range(1, cls):
-            total = total + qb[k, slot]
-        return total
+    sibling = at(col=g * 2 + 1 - h)
+
+    def sum_rows(k):
+        arrived(sib.at[k], sib_r.at[k])
+        ysum[k, g] = pq[k, :, own_h] + sib[k]
+        for dg in (2, 1, 3):
+            send(ysum.at[k, g], ysum.at[k, g], y_s.at[k], y_r.at[k], at(col=rem(g + dg, groups) * 2 + h))
 
     def dual_step(k, weight, count, eta, flag):
-        sigma = column(eta * weight, own_g, GROUP)
-        cnt = column(count, own_g, GROUP)
-        flg = column(flag, own_g, GROUP) > 0.5
-        q = receive_rows(k)
+        sigma = column(eta * weight, 0, scen)
+        cnt = column(count, 0, scen)
+        flg = column(flag, 0, scen) > 0.5
+        arrived(ysum.at[k, pl.ds(1, groups - 1)], y_r.at[k])
+        q = ysum[k, 0]
+        for i in range(1, groups):
+            q = q + ysum[k, i]
         mine = dem[...]
         if k == 0:
             nxt = jnp.maximum(sigma * (mine - 2.0 * q), 0.0)
@@ -186,10 +175,8 @@
             dual = jnp.where(flg, avg, nxt)
             anchor = danc[...]
         ds[...] = dual
-        wbuf[k, pl.ds(own_g, GROUP), pl.ds(own_h, half)] = dual
-        piece = wbuf.at[k, pl.ds(own_g, GROUP), pl.ds(own_h, half)]
-        for slot, to_g, hh, _ in col_slots():
-            send(piece, piece, agc_s.at[k], agc_r.at[k], at(col=to_g * 2 + hh))
+        wbuf[k, :, own_h] = dual
+        send(wbuf.at[k, :, own_h], wbuf.at[k, :, own_h], dual_s.at[k], dual_r.at[k], sibling)
         davg[...] = avg
         qavg[...] = qa
         q_now = jnp.where(flg, qa, q)
@@ -201,8 +188,15 @@
         violation = jnp.sum(jnp.square(jnp.maximum(mine - q_now, 0.0)), axis=1, keepdims=True)
         return violation, jnp.sum(mine * dual, axis=1, keepdims=True)
 
+    def adjoint_own(k):
+        parts = stacked(wbuf[k, :, own_h])
+        for first, size in CHUNKS:
+            part = pl.ds(first, size)
+            pa[k, :, part] = product(parts, kh[own_h, part], kl[own_h, part], NN)
+        side[k] = product(parts, lh[own_h, :], ll[own_h, :], NN)
+
     def adjoint_side(k, left):
-        side[k] = product(left, lh[...], ll[...], NN)
+        side[k] = side[k] + product(left, lh[other_h, :], ll[other_h, :], NN)
         for d in range(rws):
             to_r = rem(r + d, rws)
             src = side.at[k, pl.ds(pl.multiple_of(to_r * GROUP, GROUP), GROUP)]
@@ -210,7 +204,7 @@
 
     def adjoint_chunk(k, j, left):
         part = pl.ds(*CHUNKS[j])
-        pa[k, :, part] = product(left, kh[:, part], kl[:, part], NN)
+        pa[k, :, part] = pa[k, :, part] + product(left, kh[other_h, part], kl[other_h, part], NN)
         for d in far_first:
             to_r = rem(r + d, rws)
             src = pa.at[k, pl.ds(pl.multiple_of(to_r * GROUP, GROUP), GROUP), part]
@@ -274,15 +268,14 @@
                     term = term + product(stacked(halo[k]), lh[...], ll[...], NT)
                 pq[k] = term if j == 0 else pq[k] + term
             else:
-                for f in (1, 0):
-                    hh = pl.multiple_of((h if f == 0 else 1 - h) * half, half)
-                    some = pl.ds(hh, half)
+                for some in (other_h, own_h):
                     pq[k, :, some] = pq[k, :, some] + product(left, kh[some, part], kl[some, part], NT)
-                    send_rows_half(k, f)
+                    if some is other_h:
+                        send(pq.at[k, :, some], sib.at[k], sib_s.at[k], sib_r.at[k], sibling)
 
     def norm_start(k, dx, dy):
         place = t * 2 + h
-        near_buf[k, place] = spread(dx, own_r) + spread(dy, scen + own_g)
+        near_buf[k, place] = spread(dx, own_r) + spread(dy / groups, scen)
         for peer in near_peers():
             send(near_buf.at[k, place], near_buf.at[k, place], near_s.at[k], near_r.at[k], peer)
 
@@ -331,10 +324,11 @@
     ll[...] = low
     arrived(halo.at[0], pair_sem.at[1])
     left0 = stacked(halo[0])
-    for f in (1, 0):
-        some = pl.ds(pl.multiple_of((h if f == 0 else 1 - h) * half, half), half)
+    for some in (other_h, own_h):
         pq[0, :, some] = pq[0, :, some] + product(left0, lh[some, :], ll[some, :], NT)
-        send_rows_half(0, f)
+        if some is other_h:
+            send(pq.at[0, :, some], sib.at[0], sib_s.at[0], sib_r.at[0], sibling)
+    sum_rows(0)
     arrived(far, pair_sem.at[3])
     pl.semaphore_wait(hello, 1)
     dx = primal_rest(0, count, flag)
@@ -344,6 +338,7 @@
             eta, flag = plan(k)
             count = count + 1.0
             apply_chunks(k, column(eta / weight, 0, scen))
+            sum_rows(k)
             dx = primal_rest(k, count, flag)
             if k == ITERS - 1:
                 primal_copy = pltpu.make_async_copy(zbuf, primal_out, out_sem.at[1])
@@ -353,16 +348,17 @@
             norm_start(k, dx, dy)
         else:
             viol, dual_part = dual_step(k, weight, count, eta, flag)
-            fpart[0] = spread(viol, own_g) + spread(dual_part, scen + own_g) + spread(dx, 2 * scen + own_r)
+            fpart[0] = spread(viol / groups, 0) + spread(dual_part / groups, scen) + spread(dx, 2 * scen + own_r)
             send(fpart.at[0], fpart.at[1], pair_sem.at[4], pair_sem.at[5], at(tm=o))
-        arrived(qb.at[k, pl.ds(1, cls - 1)], agc_r.at[k])
-        dual_parts = stacked(wbuf[k])
+        adjoint_own(k)
+        arrived(wbuf.at[k, :, other_h], dual_r.at[k])
+        dual_parts = stacked(wbuf[k, :, other_h])
         for j in range(len(CHUNKS)):
             adjoint_chunk(k, j, dual_parts)
             if j == 0:
                 adjoint_side(k, dual_parts)
-                if k < ITERS - 1:
-                    norm_middle(k)
+            if j == 2 and k < ITERS - 1:
+                norm_middle(k)
         if k < ITERS - 1:
             adjoint_sums(k)
             weight = norm_weight(k, weight, flag)
@@ -386,8 +382,9 @@
     left(costs, pair_sem.at[2])
     left(fpart.at[0], pair_sem.at[4])
     for k in range(ITERS):
-        left(qb.at[k, pl.ds(1, cls - 1)], rsc_s.at[k])
-        left(qb.at[k, pl.ds(1, cls - 1)], agc_s.at[k])
+        left(sib.at[k], sib_s.at[k])
+        left(ysum.at[k, pl.ds(1, groups - 1)], y_s.at[k])
+        left(sib.at[k], dual_s.at[k])
         left(side.at[k], side_s.at[k])
         left(pa.at[k], rsr_s.at[k])
         if k > 0:
@@ -425,19 +422,19 @@
     n = ITERS
     scratch = [
         pltpu.SMEM(block_map.shape, jnp.int32), V(restart_flag.shape, jnp.int32), V(step_index.shape, jnp.int32),
-        V((GROUP, half), f32), V((2, 1, cols), f32), V((2, 1, cols), f32),
+        V((scen, half), f32), V((2, 1, cols), f32), V((2, 1, cols), f32),
         V((rows, cols), f32), V((rows, stor), f32),
         V((rows, cols), bf16), V((rows, cols), bf16), V((rows, stor), bf16), V((rows, stor), bf16),
         V((n, scen, cols), f32), V((n - 1, GROUP, cols), f32), V((n - 1, scen, cols), f32), V((n, scen, stor), f32), V((n, scen, rows), f32),
-        V((n, cls, GROUP, half), f32),
+        V((n, scen, half), f32), V((n, groups, scen, half), f32),
         V((n, scen, rows), f32), V((n, scen, cols), f32), V((n, scen, stor), f32),
         V((n, rws, GROUP, cols), f32), V((n, rws, GROUP, stor), f32), V((scen, cols), f32),
         V((scen, cols), f32), V((scen, cols), f32), V((GROUP, cols), f32),
-        V((GROUP, half), f32), V((GROUP, half), f32), V((GROUP, half), f32), V((GROUP, half), f32), V((GROUP, half), f32),
+        V((scen, half), f32), V((scen, half), f32), V((scen, half), f32), V((scen, half), f32), V((scen, half), f32),
         V((n - 1, 2 * tms, 1, LANES), f32), V((n - 1, groups * rws, 1, LANES), f32),
         V((2, 1, LANES), f32), V((1, LANES), f32), V((rws * cls, 1, LANES), f32),
         D((block_map.shape[0] + 1,)), D((6,)), D((2,)), D((6,)), pltpu.SemaphoreType.REGULAR,
-        D((n,)), D((n,)), D((n,)), D((n,)), D((n,)), D((n,)),
+        D((n,)), D((n,)), D((n,)), D((n,)), D((n,)), D((n,)), D((n,)), D((n,)),
         D((n,)), D((n,)), D((n,)), D((n, len(CHUNKS))), D((n - 1,)), D((n - 1, len(CHUNKS))),
         D((n - 1,)), D((n - 1,)), D((n - 1,)), D((n - 1,)), D((2,)),
     ]

time: 95 us -> 91.4 us (0.962)
  Pallas kernels: 92.4 us -> 88.8 us
    pallas_call x1, Pallas kernels: 92.4 us -> 88.8 us  [on_device(): pl.pallas_call(functools.partial(kernel, (tms, rws, cls)), out_shape=(jax...]
where the time goes in v5:
time: 91.4 us
  Pallas kernels  88.8 us (97%)
  local copies, waits for them, and re-layouts  1.92 us (2%)
    pallas_call x1, Pallas kernels, on_device(): pl.pallas_call(functools.partial(kernel, (tms, rws, cls)), out_shape=(jax...  88.8 us

profile of v5, /device:TPU:1, one launch (start us, length us, event | category | flops | bytes accessed | tf_op | source)
XLA Modules:
  0.0 91.4 jit_solution(8057989240892455763)
XLA Ops:
  0.6 88.8 %pdhg.1 = (f32[32,2048]{1,0:T(8,128)S(1)}, f32[32,1024]{1,0:T(8,128)S(1)}, f32[1,3,32]{2,1,0:T(4,128)S(1)}) custom-call(f32[1024,2048]{1,0:T(8,128)} %mat.1, s32[4,8]{1,0:T(4,128)} %bmap_in.1, f32[1024,256]{1,0:T(8,128)} %link.1, f32[32,1024]{1,0:T(8,128)} %dem_in.1, f32[1,2048]{1,0:T(1,128)} %bitcast.2, f32[1,2048]{1,0:T(1,128)} %bitcast.3, ...), custom_call_target="tpu_custom_call" | custom-call | tf_op jit(solution)/shard_map/pdhg/pallas_call | solution.py:441
  89.4 0.6 copy.11
  90.0 0.7 copy.14
  90.7 0.7 copy.15

commit v6 on v5

--- a/solution.py
+++ b/solution.py
@@ -152,7 +152,7 @@
         arrived(sib.at[k], sib_r.at[k])
         ysum[k, g] = pq[k, :, own_h] + sib[k]
         for dg in (2, 1, 3):
-            send(ysum.at[k, g], ysum.at[k, g], y_s.at[k], y_r.at[k], at(col=rem(g + dg, groups) * 2 + h))
+            send(ysum.at[k, g], ysum.at[k, g], y_s.at[0], y_r.at[k], at(col=rem(g + dg, groups) * 2 + h))
 
     def dual_step(k, weight, count, eta, flag):
         sigma = column(eta * weight, 0, scen)
@@ -176,7 +176,7 @@
             anchor = danc[...]
         ds[...] = dual
         wbuf[k, :, own_h] = dual
-        send(wbuf.at[k, :, own_h], wbuf.at[k, :, own_h], dual_s.at[k], dual_r.at[k], sibling)
+        send(wbuf.at[k, :, own_h], wbuf.at[k, :, own_h], dual_s.at[0], dual_r.at[k], sibling)
         davg[...] = avg
         qavg[...] = qa
         q_now = jnp.where(flg, qa, q)
@@ -200,7 +200,7 @@
         for d in range(rws):
             to_r = rem(r + d, rws)
             src = side.at[k, pl.ds(pl.multiple_of(to_r * GROUP, GROUP), GROUP)]
-            send(src, sb.at[k, d], side_s.at[k], side_r.at[k], at(tm=behind, row=to_r))
+            send(src, sb.at[k, d], side_s.at[0], side_r.at[k], at(tm=behind, row=to_r))
 
     def adjoint_chunk(k, j, left):
         part = pl.ds(*CHUNKS[j])
@@ -208,7 +208,7 @@
         for d in far_first:
             to_r = rem(r + d, rws)
             src = pa.at[k, pl.ds(pl.multiple_of(to_r * GROUP, GROUP), GROUP), part]
-            send(src, ab.at[k, d, :, part], rsr_s.at[k], rsr_r.at[k, j], at(tm=o, row=to_r))
+            send(src, ab.at[k, d, :, part], rsr_s.at[0], rsr_r.at[k, j], at(tm=o, row=to_r))
 
     def receive_adjoint(k, j):
         part = pl.ds(*CHUNKS[j])
@@ -227,7 +227,7 @@
             for d in far_first:
                 send(
                     gsum.at[k, :, part], gbuf.at[k, pl.ds(own_r, GROUP), part],
-                    agr_s.at[k], agr_r.at[k, j], at(tm=o, row=rem(r + d, rws)),
+                    agr_s.at[0], agr_r.at[k, j], at(tm=o, row=rem(r + d, rws)),
                 )
 
     def primal_rest(k, count, flag):
@@ -260,7 +260,7 @@
             ybuf[k, :, part] = nxt
             left = stacked(nxt)
             if CHUNKS[j][0] == edge:
-                send(ybuf.at[k, :, part], halo.at[k], halo_s.at[k], halo_r.at[k], at(tm=rem(t + 1, tms)))
+                send(ybuf.at[k, :, part], halo.at[k], halo_s.at[0], halo_r.at[k], at(tm=rem(t + 1, tms)))
             if j != final:
                 term = product(left, kh[:, part], kl[:, part], NT)
                 if j == final - 1:
@@ -271,13 +271,13 @@
                 for some in (other_h, own_h):
                     pq[k, :, some] = pq[k, :, some] + product(left, kh[some, part], kl[some, part], NT)
                     if some is other_h:
-                        send(pq.at[k, :, some], sib.at[k], sib_s.at[k], sib_r.at[k], sibling)
+                        send(pq.at[k, :, some], sib.at[k], sib_s.at[0], sib_r.at[k], sibling)
 
     def norm_start(k, dx, dy):
         place = t * 2 + h
         near_buf[k, place] = spread(dx, own_r) + spread(dy / groups, scen)
         for peer in near_peers():
-            send(near_buf.at[k, place], near_buf.at[k, place], near_s.at[k], near_r.at[k], peer)
+            send(near_buf.at[k, place], near_buf.at[k, place], near_s.at[0], near_r.at[k], peer)
 
     def norm_middle(k):
         arrived(near_buf.at[k, pl.ds(1, 2 * tms - 1)], near_r.at[k])
@@ -287,7 +287,7 @@
         place = r * groups + g
         wide_buf[k, place] = total
         for peer in wide_peers():
-            send(wide_buf.at[k, place], wide_buf.at[k, place], wide_s.at[k], wide_r.at[k], peer)
+            send(wide_buf.at[k, place], wide_buf.at[k, place], wide_s.at[0], wide_r.at[k], peer)
 
     def norm_weight(k, weight, flag):
         arrived(wide_buf.at[k, pl.ds(1, groups * rws - 1)], wide_r.at[k])
@@ -381,18 +381,15 @@
     left(halo.at[0], pair_sem.at[0])
     left(costs, pair_sem.at[2])
     left(fpart.at[0], pair_sem.at[4])
-    for k in range(ITERS):
-        left(sib.at[k], sib_s.at[k])
-        left(ysum.at[k, pl.ds(1, groups - 1)], y_s.at[k])
-        left(sib.at[k], dual_s.at[k])
-        left(side.at[k], side_s.at[k])
-        left(pa.at[k], rsr_s.at[k])
-        if k > 0:
-            left(gbuf.at[k - 1], agr_s.at[k - 1])
-            left(halo.at[k], halo_s.at[k])
-        if k < ITERS - 1:
-            left(near_buf.at[k, pl.ds(1, 2 * tms - 1)], near_s.at[k])
-            left(wide_buf.at[k, pl.ds(1, groups * rws - 1)], wide_s.at[k])
+    left(sib, sib_s.at[0])
+    left(ysum.at[:, pl.ds(1, groups - 1)], y_s.at[0])
+    left(sib, dual_s.at[0])
+    left(side, side_s.at[0])
+    left(pa, rsr_s.at[0])
+    left(gbuf, agr_s.at[0])
+    left(halo.at[pl.ds(1, ITERS - 1)], halo_s.at[0])
+    left(near_buf.at[:, pl.ds(1, 2 * tms - 1)], near_s.at[0])
+    left(wide_buf.at[:, pl.ds(1, groups * rws - 1)], wide_s.at[0])
     left(fall, fall_sem.at[0])
     dual_copy.wait()
     primal_copy.wait()
@@ -402,9 +399,9 @@
         total = total + fall[i]
     con_total, var_total = float(rows * rws), float(cols * cls)
     parts = [total[:, i * scen : (i + 1) * scen] for i in range(4)]
-    kkt_out[0, 0:1, :] = jnp.sqrt(parts[0] / con_total + 1e-06)
-    kkt_out[0, 1:2, :] = parts[2] / var_total
-    kkt_out[0, 2:3, :] = (parts[1] + parts[3]) / var_total
+    kkt_out[0] = jnp.sqrt(parts[0] / con_total + 1e-06)
+    kkt_out[1] = parts[2] / var_total
+    kkt_out[2] = (parts[1] + parts[3]) / var_total
 
 
 def on_device(matrix_tiles, block_map, link_tiles, demand, objective, upper_bound, restart_flag, step_index):
@@ -434,16 +431,16 @@
         V((n - 1, 2 * tms, 1, LANES), f32), V((n - 1, groups * rws, 1, LANES), f32),
         V((2, 1, LANES), f32), V((1, LANES), f32), V((rws * cls, 1, LANES), f32),
         D((block_map.shape[0] + 1,)), D((6,)), D((2,)), D((6,)), pltpu.SemaphoreType.REGULAR,
-        D((n,)), D((n,)), D((n,)), D((n,)), D((n,)), D((n,)), D((n,)), D((n,)),
-        D((n,)), D((n,)), D((n,)), D((n, len(CHUNKS))), D((n - 1,)), D((n - 1, len(CHUNKS))),
-        D((n - 1,)), D((n - 1,)), D((n - 1,)), D((n - 1,)), D((2,)),
+        D((1,)), D((n,)), D((1,)), D((n,)), D((1,)), D((n,)), D((1,)), D((n,)),
+        D((1,)), D((n,)), D((1,)), D((n, len(CHUNKS))), D((1,)), D((n - 1, len(CHUNKS))),
+        D((1,)), D((n - 1,)), D((1,)), D((n - 1,)), D((2,)),
     ]
-    return pl.pallas_call(
+    primal, dual, kkt = pl.pallas_call(
         functools.partial(kernel, (tms, rws, cls)),
         out_shape=(
             jax.ShapeDtypeStruct((scen, cols), f32),
             jax.ShapeDtypeStruct((scen, rows), f32),
-            jax.ShapeDtypeStruct((1, 3, scen), f32),
+            jax.ShapeDtypeStruct((3, 1, scen), f32),
         ),
         in_specs=[hbm] * 8,
         out_specs=(hbm, hbm, vmem),
@@ -459,6 +456,7 @@
             restart_flag, step_index,
         )
     ))
+    return primal, dual, kkt.transpose(1, 0, 2)
 
 
 def solution(mesh):

time: 91.4 us -> 91.3 us (level)
    unnamed x2 -> x3, local copies, waits for them, and re-layouts: 1.36 us -> 1.92 us
where the time goes in v6:
time: 91.3 us; the launch traced here: 91.2 us
  Pallas kernels  88.7 us (97%)
  local copies, waits for them, and re-layouts  1.92 us (2%)
    pallas_call x1, Pallas kernels, on_device(): pl.pallas_call(functools.partial(kernel, (tms, rws, cls)), out_shape=(jax...  88.7 us
    unnamed x3, local copies, waits for them, and re-layouts  1.92 us

profile of v6, /device:TPU:1, one launch (start us, length us, event | category | flops | bytes accessed | tf_op | source)
XLA Modules:
  0.0 91.2 jit_solution(17475581821026795021)
XLA Ops:
  0.6 88.7 %pdhg.1 = (f32[32,2048]{1,0:T(8,128)S(1)}, f32[32,1024]{1,0:T(8,128)S(1)}, f32[3,1,32]{2,1,0:T(1,128)S(1)}) custom-call(f32[1024,2048]{1,0:T(8,128)} %mat.1, s32[4,8]{1,0:T(4,128)} %bmap_in.1, f32[1024,256]{1,0:T(8,128)} %link.1, f32[32,1024]{1,0:T(8,128)} %dem_in.1, f32[1,2048]{1,0:T(1,128)} %bitcast.4, f32[1,2048]{1,0:T(1,128)} %bitcast.5, ...), custom_call_target="tpu_custom_call" | custom-call | tf_op jit(solution)/shard_map/pdhg/pallas_call | solution.py:438
  89.3 0.7 copy.14
  90.0 0.7 copy.15
  90.7 0.6 copy.16
